TPU v7x, 256 devices: a whole 4x4x8 slice. The times are simulated.
256 devices in a mesh: pipe: 8 (over x, core), expert: 32 (over y, z).
Axes of the slice: x: 4, y: 4, z: 8, core: 2. Of those that a mesh axis runs over, the one named last changes fastest.
Arguments:
- stream_fwd: bfloat16 [8, 4096, 3584], P('pipe', 'expert'), may hold values from -6 to 6
- stream_rev: bfloat16 [8, 4096, 3584], P('pipe', 'expert'), may hold values from -6 to 6
- norm_gain: bfloat16 [8, 3584], P('pipe'), may hold values from 0.099609375 to 1.8984375
- w_up: bfloat16 [8, 32, 3584, 512], P('pipe', 'expert'), may hold values from -0.09375 to 0.09375
- w_down: bfloat16 [8, 32, 512, 3584], P('pipe', 'expert'), may hold values from -0.1875 to 0.1875
- routes: int32 [8, 2, 4096, 2], P('pipe', None, 'expert'), may hold values from 0 to 15, all different within a row; in each aligned block of 128 rows (0 to 127, 128 to 255, ..., all dimensions but the last counted through in order) at most 20 rows name the same one
- gates: bfloat16 [8, 2, 4096, 2], P('pipe', None, 'expert'), may hold values from 0.19921875 to 1
Outputs:
- next_fwd: bfloat16 [8, 4096, 3584], P('pipe', 'expert')
- next_rev: bfloat16 [8, 4096, 3584], P('pipe', 'expert')
Inputs may be any that keep to these rules, and one draw needn't show every extreme that they name: `routes`: each row names 2 different experts; among the 128 rows of one device for one section and direction no expert is named more than 20 times, a bound that some block reaches.
All inputs are finite; a program needn't handle non-finite values.
Results may differ from a plain program's by a relative error of at most 0.012.
Values may be sent and summed in bfloat16 or wider, within the bound.
A program may use at most 128 MiB of HBM per device.

v0:
```python
import jax
import jax.numpy as jnp
from jax import lax
from jax.sharding import PartitionSpec as P

SPLIT = 2
TOPK = 2


def shifted(block, axis, distance):
    devices = range(lax.axis_size(axis))
    route = [((i - distance) % len(devices), i) for i in devices]
    return lax.ppermute(block, axis, route)


def expert_rows(rows, upper, lower):
    hidden = jax.nn.silu(jnp.dot(rows, upper, preferred_element_type=jnp.float32)).astype(
        jnp.bfloat16
    )
    return jnp.dot(hidden, lower, preferred_element_type=jnp.float32).astype(jnp.bfloat16)


def moe_layer(x, gain, upper, lower, idx, gval):
    devices = lax.axis_size("expert")
    experts = devices // SPLIT
    tok = x.shape[0]
    width = x.shape[1]
    cap = SPLIT * max(1, tok * TOPK * 5 // (4 * SPLIT * experts))
    xf = x.astype(jnp.float32)
    scale = lax.rsqrt(jnp.mean(xf * xf, axis=-1, keepdims=True) + 1e-06)
    normed = (xf * scale * gain.astype(jnp.float32)).astype(jnp.bfloat16)
    picks = idx.reshape(-1)
    match = picks[:, None] == jnp.arange(experts, dtype=jnp.int32)[None, :]
    ranks = jnp.cumsum(match.astype(jnp.int32), axis=0) - 1
    slots = jnp.sum(jnp.where(match, ranks, 0), axis=-1)
    target = picks * cap + slots
    placed = target[:, None] == jnp.arange(experts * cap, dtype=jnp.int32)[None, :]
    placed = placed.reshape(tok, TOPK, experts * cap)
    spread = jnp.any(placed, axis=1).astype(jnp.bfloat16)
    weights = jnp.where(placed, gval[:, :, None], jnp.zeros((), jnp.bfloat16))
    combiner = jnp.sum(weights.astype(jnp.float32), axis=1).astype(jnp.bfloat16)
    buffer = jnp.einsum("tc,td->cd", spread, normed, preferred_element_type=jnp.float32).astype(
        jnp.bfloat16
    )
    outgoing = jnp.repeat(buffer.reshape(experts, cap, width), SPLIT, axis=0)
    incoming = lax.all_to_all(outgoing, "expert", split_axis=0, concat_axis=0, tiled=True)
    partial_value = expert_rows(incoming.reshape(devices * cap, width), upper, lower)
    returned = lax.all_to_all(
        partial_value.reshape(devices, cap, width),
        "expert",
        split_axis=0,
        concat_axis=0,
        tiled=True,
    )
    paired = returned.reshape(experts, SPLIT, cap, width).astype(jnp.float32)
    expert_out = (paired[:, 0] + paired[:, 1]).astype(jnp.bfloat16)
    mixed = xf + jnp.dot(
        combiner, expert_out.reshape(experts * cap, width), preferred_element_type=jnp.float32
    )
    return mixed.astype(jnp.bfloat16)


def shards(stream_fwd, stream_rev, norm_gain, w_up, w_down, routes, gates):
    gain = norm_gain[0]
    upper = w_up[0, 0]
    lower = w_down[0, 0]
    forward_out = moe_layer(stream_fwd[0], gain, upper, lower, routes[0, 0], gates[0, 0])
    reverse_out = moe_layer(stream_rev[0], gain, upper, lower, routes[0, 1], gates[0, 1])
    next_fwd = shifted(forward_out[None], "pipe", 1)
    next_rev = shifted(reverse_out[None], "pipe", -1)
    return (next_fwd, next_rev)


def solution(mesh):
    return jax.shard_map(
        shards,
        mesh=mesh,
        in_specs=(
            P("pipe", "expert", None),
            P("pipe", "expert", None),
            P("pipe", None),
            P("pipe", "expert", None, None),
            P("pipe", "expert", None, None),
            P("pipe", None, "expert", None),
            P("pipe", None, "expert", None),
        ),
        out_specs=(P("pipe", "expert", None), P("pipe", "expert", None)),
        check_vma=False,
    )
```

profile of v0, /device:TPU:1, one launch (start us, length us, event | category | flops | bytes accessed | tf_op | source)
XLA Modules:
  0.0 572.2 jit_solution(1355886812338574891)
XLA Ops:
  0.6 0.7 fusion.44
  1.6 0.1 eq.89
  1.7 0.6 reduce-window.16
  2.3 0.2 slice_reduce_fusion
  2.6 0.1 reduce_sum.69
  2.9 0.8 convert_reduce_fusion
  3.7 1.4 fusion.17
  5.2 2.0 convolution_convert_fusion.2
  7.2 2.2 reshape.150
  9.4 4.6 broadcast_in_dim.57
  14.0 12.3 %all-to-all-start.2 = ((bf16[32,20,3584]{2,1,0:T(8,128)(2,1)}), bf16[32,20,3584]{2,1,0:T(8,128)(2,1)}, u32[]{:S(2)}, u32[]{:S(2)}) async-start(bf16[32,20,3584]{2,1,0:T(8,128)(2,1)} %bitcast.120), calls=%async_computation.2 | async-start | bytes 11010048 | tf_op jit(solution)/shard_map/all_to_all | solution.py:46
  26.4 0.1 eq.82
  26.6 0.1 eq.78
  26.7 0.6 reduce-window.14
  27.3 0.2 slice_reduce_fusion.1
  27.6 0.1 reduce_sum.65
  27.9 0.3 fusion.14
  28.2 0.8 convolution_convert_fusion.3
  29.1 2.2 reshape.145
  31.3 117.5 %all-to-all-done.2 = bf16[32,20,3584]{2,1,0:T(8,128)(2,1)} async-done(((bf16[32,20,3584]{2,1,0:T(8,128)(2,1)}), bf16[32,20,3584]{2,1,0:T(8,128)(2,1)}, u32[]{:S(2)}, u32[]{:S(2)}) %all-to-all-start.2) | async-done | bytes 4587552 | tf_op jit(solution)/shard_map/all_to_all | solution.py:46
  148.8 4.6 broadcast_in_dim.53
  153.4 8.9 %all-to-all-start = ((bf16[32,20,3584]{2,1,0:T(8,128)(2,1)}), bf16[32,20,3584]{2,1,0:T(8,128)(2,1)}, u32[]{:S(2)}, u32[]{:S(2)}) async-start(bf16[32,20,3584]{2,1,0:T(8,128)(2,1)} %bitcast.121), calls=%async_computation | async-start | bytes 11010048 | tf_op jit(solution)/shard_map/all_to_all | solution.py:46
  162.3 7.3 %reshape.152 = bf16[640,3584]{1,0:T(8,128)(2,1)} reshape(bf16[32,20,3584]{2,1,0:T(8,128)(2,1)} %all-to-all-done.2) | data formatting | bytes 9175040 | tf_op jit(solution)/shard_map/reshape | solution.py:47
  169.5 6.3 %multiply_convert_fusion = bf16[640,512]{1,0:T(8,128)(2,1)S(1)} fusion(bf16[640,3584]{1,0:T(8,128)(2,1)} %reshape.152, bf16[1,1,3584,512]{3,2,1,0:T(8,128)(2,1)} %param.10), kind=kOutput, calls=%fused_computation.34 | convolution fusion | flops 2350448640 | bytes 8912896 | tf_op jit(solution)/shard_map/dot_general | solution.py:17
  175.8 4.6 convolution_convert_fusion
  180.4 7.3 %reshape.153 = bf16[32,20,3584]{2,1,0:T(8,128)(2,1)} reshape(bf16[640,3584]{1,0:T(8,128)(2,1)} %convolution_convert_fusion) | data formatting | bytes 9175040 | tf_op jit(solution)/shard_map/reshape | solution.py:49
  187.7 97.0 %all-to-all-done = bf16[32,20,3584]{2,1,0:T(8,128)(2,1)} async-done(((bf16[32,20,3584]{2,1,0:T(8,128)(2,1)}), bf16[32,20,3584]{2,1,0:T(8,128)(2,1)}, u32[]{:S(2)}, u32[]{:S(2)}) %all-to-all-start) | async-done | bytes 4587552 | tf_op jit(solution)/shard_map/all_to_all | solution.py:46
  284.8 8.6 %all-to-all-start.3 = ((bf16[32,20,3584]{2,1,0:T(8,128)(2,1)}), bf16[32,20,3584]{2,1,0:T(8,128)(2,1)}, u32[]{:S(2)}, u32[]{:S(2)}) async-start(bf16[32,20,3584]{2,1,0:T(8,128)(2,1)} %reshape.153), calls=%async_computation.3 | async-start | bytes 11010048 | tf_op jit(solution)/shard_map/all_to_all | solution.py:48
  293.3 7.3 %reshape.147 = bf16[640,3584]{1,0:T(8,128)(2,1)} reshape(bf16[32,20,3584]{2,1,0:T(8,128)(2,1)} %all-to-all-done) | data formatting | bytes 9175040 | tf_op jit(solution)/shard_map/reshape | solution.py:47
  300.6 6.3 %multiply_convert_fusion.1 = bf16[640,512]{1,0:T(8,128)(2,1)S(1)} fusion(bf16[640,3584]{1,0:T(8,128)(2,1)} %reshape.147, bf16[1,1,3584,512]{3,2,1,0:T(8,128)(2,1)} %param.10), kind=kOutput, calls=%fused_computation.35 | convolution fusion | flops 2350448640 | bytes 8912896 | tf_op jit(solution)/shard_map/dot_general | solution.py:17
  306.9 4.6 convolution_convert_fusion.1
  311.5 7.2 %reshape.148 = bf16[32,20,3584]{2,1,0:T(8,128)(2,1)} reshape(bf16[640,3584]{1,0:T(8,128)(2,1)} %convolution_convert_fusion.1) | data formatting | bytes 9175040 | tf_op jit(solution)/shard_map/reshape | solution.py:49
  318.7 97.3 %all-to-all-done.3 = bf16[32,20,3584]{2,1,0:T(8,128)(2,1)} async-done(((bf16[32,20,3584]{2,1,0:T(8,128)(2,1)}), bf16[32,20,3584]{2,1,0:T(8,128)(2,1)}, u32[]{:S(2)}, u32[]{:S(2)}) %all-to-all-start.3) | async-done | bytes 4587552 | tf_op jit(solution)/shard_map/all_to_all | solution.py:48
  416.0 8.2 %all-to-all-start.1 = ((bf16[32,20,3584]{2,1,0:T(8,128)(2,1)}), bf16[32,20,3584]{2,1,0:T(8,128)(2,1)}, u32[]{:S(2)}, u32[]{:S(2)}) async-start(bf16[32,20,3584]{2,1,0:T(8,128)(2,1)} %reshape.148), calls=%async_computation.1 | async-start | bytes 11010048 | tf_op jit(solution)/shard_map/all_to_all | solution.py:48
  424.3 4.0 convert.10
  428.4 0.7 fusion.1
  429.0 2.1 convert_element_type.109
  431.2 3.5 fusion.6
  434.6 0.8 collective-permute-start.1
  435.4 111.5 %all-to-all-done.1 = bf16[32,20,3584]{2,1,0:T(8,128)(2,1)} async-done(((bf16[32,20,3584]{2,1,0:T(8,128)(2,1)}), bf16[32,20,3584]{2,1,0:T(8,128)(2,1)}, u32[]{:S(2)}, u32[]{:S(2)}) %all-to-all-start.1) | async-done | bytes 4587552 | tf_op jit(solution)/shard_map/all_to_all | solution.py:48
  546.9 4.0 convert.8
  550.9 0.7 fusion.3
  551.6 2.1 convert_element_type.97
  553.7 2.5 fusion.7
  556.3 2.6 collective-permute-start
  558.8 10.3 %collective-permute-done = bf16[1,128,3584]{2,1,0:T(8,128)(2,1)S(1)} collective-permute-done((bf16[1,128,3584]{2,1,0:T(8,128)(2,1)S(1)}, bf16[1,128,3584]{2,1,0:T(8,128)(2,1)S(1)}, u32[]{:S(2)}, u32[]{:S(2)}) %collective-permute-start) | collective-permute-done | bytes 917536 | tf_op jit(solution)/shard_map/ppermute | solution.py:13
  569.2 0.9 copy.45
  570.1 2.2 copy.46
  (31 shorter events, 1.0 us)
Async XLA Ops:
  14.0 13.9 %copy-start = (bf16[1,128,3584]{2,1,0:T(8,128)(2,1)S(1)}, bf16[1,128,3584]{2,1,0:T(8,128)(2,1)}, u32[]{:S(2)}) copy-start(bf16[1,128,3584]{2,1,0:T(8,128)(2,1)} %param.7) | copy-start | bytes 2752516
  14.0 134.8 %all-to-all-start.2 = ((bf16[32,20,3584]{2,1,0:T(8,128)(2,1)}), bf16[32,20,3584]{2,1,0:T(8,128)(2,1)}, u32[]{:S(2)}, u32[]{:S(2)}) async-start(bf16[32,20,3584]{2,1,0:T(8,128)(2,1)} %bitcast.120), calls=%async_computation.2 | async-start | bytes 11010048 | tf_op jit(solution)/shard_map/all_to_all | solution.py:46
  153.4 131.4 %all-to-all-start = ((bf16[32,20,3584]{2,1,0:T(8,128)(2,1)}), bf16[32,20,3584]{2,1,0:T(8,128)(2,1)}, u32[]{:S(2)}, u32[]{:S(2)}) async-start(bf16[32,20,3584]{2,1,0:T(8,128)(2,1)} %bitcast.121), calls=%async_computation | async-start | bytes 11010048 | tf_op jit(solution)/shard_map/all_to_all | solution.py:46
  169.5 6.3 %copy-start.2 = (bf16[1,1,512,3584]{3,2,1,0:T(8,128)(2,1)S(1)}, bf16[1,1,512,3584]{3,2,1,0:T(8,128)(2,1)}, u32[]{:S(2)}) copy-start(bf16[1,1,512,3584]{3,2,1,0:T(8,128)(2,1)} %param.11) | copy-start | bytes 11010052
  284.8 131.3 %all-to-all-start.3 = ((bf16[32,20,3584]{2,1,0:T(8,128)(2,1)}), bf16[32,20,3584]{2,1,0:T(8,128)(2,1)}, u32[]{:S(2)}, u32[]{:S(2)}) async-start(bf16[32,20,3584]{2,1,0:T(8,128)(2,1)} %reshape.153), calls=%async_computation.3 | async-start | bytes 11010048 | tf_op jit(solution)/shard_map/all_to_all | solution.py:48
  300.6 6.3 %copy-start.3 = (bf16[1,1,512,3584]{3,2,1,0:T(8,128)(2,1)S(1)}, bf16[1,1,512,3584]{3,2,1,0:T(8,128)(2,1)}, u32[]{:S(2)}) copy-start(bf16[1,1,512,3584]{3,2,1,0:T(8,128)(2,1)} %param.11) | copy-start | bytes 11010052
  318.7 105.5 %copy-start.1 = (bf16[1,2,128,2]{2,3,1,0:T(2,128)(2,1)S(1)}, bf16[1,2,128,2]{2,3,1,0:T(2,128)(2,1)}, u32[]{:S(2)}) copy-start(bf16[1,2,128,2]{2,3,1,0:T(2,128)(2,1)} %param.13) | copy-start | bytes 3076
  416.0 130.9 %all-to-all-start.1 = ((bf16[32,20,3584]{2,1,0:T(8,128)(2,1)}), bf16[32,20,3584]{2,1,0:T(8,128)(2,1)}, u32[]{:S(2)}, u32[]{:S(2)}) async-start(bf16[32,20,3584]{2,1,0:T(8,128)(2,1)} %reshape.148), calls=%async_computation.1 | async-start | bytes 11010048 | tf_op jit(solution)/shard_map/all_to_all | solution.py:48
  434.6 124.2 %collective-permute-start.1 = (bf16[1,128,3584]{2,1,0:T(8,128)(2,1)}, bf16[1,128,3584]{2,1,0:T(8,128)(2,1)}, u32[]{:S(2)}, u32[]{:S(2)}) collective-permute-start(bf16[1,128,3584]{2,1,0:T(8,128)(2,1)} %fusion.6), channel_id=1, source_target_pairs={{32,0},{64,32},{96,64},{128,96},{160,128},{192,160},{224,192},{0,2... | collective-permute-start | bytes 2752520 | tf_op jit(solution)/shard_map/ppermute | solution.py:13
  556.3 12.9 %collective-permute-start = (bf16[1,128,3584]{2,1,0:T(8,128)(2,1)S(1)}, bf16[1,128,3584]{2,1,0:T(8,128)(2,1)S(1)}, u32[]{:S(2)}, u32[]{:S(2)}) collective-permute-start(bf16[1,128,3584]{2,1,0:T(8,128)(2,1)S(1)} %fusion.7), channel_id=1, source_target_pairs={{224,0},{0,32},{32,64},{64,96},{96,128},{128,160},{160,192},{192,2... | collective-permute-start | bytes 2752520 | tf_op jit(solution)/shard_map/ppermute | solution.py:13
where the time goes:
time: 575 us; the launch traced here: 572 us
  waiting for transfers between devices  434 us (75%)
  local copies, waits for them, and re-layouts  52.3 us (9%)
  starting transfers between devices  41.2 us (7%)
  matrix products  30.6 us (5%)
  other arithmetic  13.5 us (2%)
    all_to_all x2, waiting for transfers between devices, moe_layer(): lax.all_to_all(outgoing, 'expert', split_axis=0, concat_axis=0, tiled=True)  215 us
    all_to_all x2, waiting for transfers between devices, moe_layer(): lax.all_to_all(partial_value.reshape(devices, cap, width), 'expert', spli...  209 us
    all_to_all x2, starting transfers between devices, moe_layer(): lax.all_to_all(outgoing, 'expert', split_axis=0, concat_axis=0, tiled=True)  21.2 us
    all_to_all x2, starting transfers between devices, moe_layer(): lax.all_to_all(partial_value.reshape(devices, cap, width), 'expert', spli...  16.7 us
    reshape x2, local copies, waits for them, and re-layouts, moe_layer(): partial_value.reshape(devices, cap, width)  14.5 us
    reshape x2, local copies, waits for them, and re-layouts, moe_layer(): incoming.reshape(devices * cap, width)  14.5 us
    dot_general x2, matrix products, expert_rows(): jnp.dot(rows, upper, preferred_element_type=jnp.float32)  12.5 us
  transfers between devices with their start and end apart: 6, of which 5 were waited for; matrix products, arithmetic and copies ran while one was open for 13% of the time, Pallas kernels for 0%

commit v1 on v0

v1 whole, which is shorter than its diff:
```python
import functools

import jax
import jax.numpy as jnp
from jax import lax
from jax.experimental import pallas as pl
from jax.experimental.pallas import tpu as pltpu
from jax.sharding import PartitionSpec as P

SPLIT = 2
TOPK = 2
NY = 4
NZ = 8
GROUP = 4
MESH = pl.DeviceIdType.MESH

POS = {0: 0, -1: 1, 1: 2, 2: 3, -2: 4, -3: 5, 3: 6, 4: 7}
LEFT, RIGHT = 0, 1


def tile_of(width, most=512):
    tile = 128
    for t in range(128, most + 1, 128):
        if width % t == 0:
            tile = t
    return tile


def kernel(
    cap,
    xf_hbm, xr_hbm, gain_ref, up_hbm, down_hbm, info_ref,
    outf_ref, outr_ref,
    ag, inc, sel, ret, relay, infos, xs, stage, up, down, act, hid, gmat,
    ag_send, ag_recv, inf_send, inf_recv, yd_send, yd_recv, yr_send, yr_recv,
    rs_send, rs_recv, sh_send, sh_recv, load_sem, credit,
):
    tok, width = xs.shape[1], xs.shape[2]
    half = width // 2
    quarter = width // 4
    rows = GROUP * cap
    p = lax.axis_index("pipe")
    e = lax.axis_index("expert")
    n_pipe = lax.axis_size("pipe")
    y, z = e // NZ, e % NZ
    m = z // SPLIT
    zdev = {RIGHT: (p, y * NZ + (z + 1) % NZ), LEFT: (p, y * NZ + (z + NZ - 1) % NZ)}
    ydev = {RIGHT: (p, ((y + 1) % NY) * NZ + z), LEFT: (p, ((y + NY - 1) % NY) * NZ + z)}
    pdev = {0: ((p + 1) % n_pipe, e), 1: ((p + n_pipe - 1) % n_pipe, e)}
    outs = {0: outf_ref, 1: outr_ref}

    def remote(src, dst, send, recv, device):
        return pltpu.make_async_remote_copy(
            src_ref=src, dst_ref=dst, send_sem=send, recv_sem=recv,
            device_id=device, device_id_type=MESH,
        )

    barrier = pltpu.get_barrier_semaphore()
    for device in (zdev[0], zdev[1], ydev[0], ydev[1], pdev[0], pdev[1]):
        pl.semaphore_signal(barrier, inc=1, device_id=device, device_id_type=MESH)

    loads = [
        pltpu.make_async_copy(xf_hbm, xs.at[0], load_sem.at[0]),
        pltpu.make_async_copy(xr_hbm, xs.at[1], load_sem.at[1]),
        pltpu.make_async_copy(up_hbm, up, load_sem.at[2]),
        pltpu.make_async_copy(down_hbm, down, load_sem.at[3]),
    ]
    for load in loads:
        load.start()

    def normalise(s):
        gain = gain_ref[...].astype(jnp.float32)

        def body(i, carry):
            at = pl.ds(pl.multiple_of(i * 16, 16), 16)
            x = xs[s, at, :].astype(jnp.float32)
            scale = lax.rsqrt(jnp.mean(x * x, axis=-1, keepdims=True) + 1e-06)
            ag[s, 0, at, :] = (x * scale * gain).astype(jnp.bfloat16)
            return carry

        lax.fori_loop(0, tok // 16, body, 0)

    def ag_copy(s, way, hop, c):
        sign = -1 if way == RIGHT else 1
        source, target = sign * (hop - 1), sign * hop
        source, target = POS[source], POS[4 if abs(target) == 4 else target]
        cols = pl.ds(c * half, half)
        return remote(
            ag.at[s, source, :, cols], ag.at[s, target, :, cols],
            ag_send.at[s, way, hop - 1, c], ag_recv.at[s, way, hop - 1, c], zdev[way],
        )

    def inf_copy(way, hop):
        sign = -1 if way == RIGHT else 1
        source, target = sign * (hop - 1), sign * hop
        source, target = POS[source], POS[4 if abs(target) == 4 else target]
        return remote(
            infos.at[source], infos.at[target],
            inf_send.at[way, hop - 1], inf_recv.at[way, hop - 1], zdev[way],
        )

    def ag_parts(way, hop):
        if hop < 4:
            return (0, 1)
        return (0,) if way == RIGHT else (1,)

    def inf_ways(hop):
        return (RIGHT, LEFT) if hop < 4 else (RIGHT,)

    def gather_hop(s, hop):
        if s == 0:
            for way in inf_ways(hop):
                if hop > 1:
                    inf_copy(way, hop - 1).wait_recv()
                inf_copy(way, hop).start()
        for c in (0, 1):
            for way in (RIGHT, LEFT):
                if hop > 1:
                    ag_copy(s, way, hop - 1, c).wait_recv()
                if c in ag_parts(way, hop):
                    ag_copy(s, way, hop, c).start()

    def gather_end(s):
        if s == 0:
            inf_copy(RIGHT, 4).wait_recv()
            inf_copy(LEFT, 3).wait_recv()
            for hop in (1, 2, 3, 4):
                for way in inf_ways(hop):
                    inf_copy(way, hop).wait_send()
        for way in (RIGHT, LEFT):
            for c in ag_parts(way, 4):
                ag_copy(s, way, 4, c).wait_recv()

    def gather_sent(s):
        for hop in (1, 2, 3, 4):
            for way in (RIGHT, LEFT):
                for c in ag_parts(way, hop):
                    ag_copy(s, way, hop, c).wait_send()

    def row_codes(shape):
        r = lax.broadcasted_iota(jnp.int32, shape, 0)
        one, zero = jnp.int32(1), jnp.int32(0)
        d = sum(jnp.where(r >= k * rows, one, zero) for k in (1, 2, 3))
        r = r - d * rows
        i = sum(jnp.where(r >= k * cap, one, zero) for k in (1, 2, 3))
        c = r - i * cap
        yd = y + d
        yd = yd - jnp.where(yd >= NY, NY * one, zero)
        expert = yd * (NZ // SPLIT) + m
        return ((i * NY * (NZ // SPLIT) + expert) * cap + c).astype(jnp.float32)

    per_source = NY * (NZ // SPLIT) * cap

    def select(s, g):
        codes = row_codes((NY * rows, tok))
        parts = []
        for i in range(GROUP):
            info = infos[GROUP * g + i]
            hit0 = codes == info[4 * s : 4 * s + 1, :] + float(i * per_source)
            hit1 = codes == info[4 * s + 1 : 4 * s + 2, :] + float(i * per_source)
            parts.append(jnp.where(hit0 | hit1, 1.0, 0.0).astype(jnp.bfloat16))
            weights = jnp.where(hit0, info[4 * s + 2 : 4 * s + 3, :], 0.0) + jnp.where(
                hit1, info[4 * s + 3 : 4 * s + 4, :], 0.0
            )
            gmat[s, GROUP * g + i] = weights.T.astype(jnp.bfloat16)
        pick = jnp.concatenate(parts, axis=1)
        tile = tile_of(width)

        def body(j, carry):
            cols = pl.ds(pl.multiple_of(j * tile, 128), tile)
            block = ag[s, GROUP * g : GROUP * (g + 1), :, cols].reshape(GROUP * tok, tile)
            out = jnp.dot(pick, block, preferred_element_type=jnp.float32).astype(jnp.bfloat16)
            inc[s, g, 0:rows, cols] = out[0:rows]
            sel[s, g, :, cols] = out[rows:]
            return carry

        lax.fori_loop(0, width // tile, body, 0)

    low, high = pl.ds(0, half), pl.ds(half, half)

    def at(d):
        return pl.ds(d * rows, rows)

    def yd_copies(s, g):
        ss, rr = yd_send.at[s, g], yd_recv.at[s, g]
        source, into, hop = sel.at[s, g], inc.at[s, g], relay.at[s, g, 0]
        first = [
            remote(source.at[at(1), low], hop.at[0], ss.at[0], rr.at[0], ydev[RIGHT]),
            remote(source.at[at(1), high], hop.at[1], ss.at[1], rr.at[1], ydev[LEFT]),
        ]
        direct = [
            remote(source.at[at(0)], into.at[at(1)], ss.at[2], rr.at[2], ydev[RIGHT]),
            remote(source.at[at(2)], into.at[at(3)], ss.at[3], rr.at[3], ydev[LEFT]),
        ]
        second = [
            remote(hop.at[0], into.at[at(2), low], ss.at[4], rr.at[4], ydev[RIGHT]),
            remote(hop.at[1], into.at[at(2), high], ss.at[5], rr.at[5], ydev[LEFT]),
        ]
        return first, direct, second

    def yr_copies(s, g):
        ss, rr = yr_send.at[s, g], yr_recv.at[s, g]
        source, into, hop = inc.at[s, g], ret.at[s, g], relay.at[s, g, 1]
        first = [
            remote(source.at[at(2), low], hop.at[0], ss.at[0], rr.at[0], ydev[LEFT]),
            remote(source.at[at(2), high], hop.at[1], ss.at[1], rr.at[1], ydev[RIGHT]),
        ]
        direct = [
            remote(source.at[at(1)], into.at[at(1)], ss.at[2], rr.at[2], ydev[LEFT]),
            remote(source.at[at(3)], into.at[at(3)], ss.at[3], rr.at[3], ydev[RIGHT]),
        ]
        second = [
            remote(hop.at[0], into.at[at(2), low], ss.at[4], rr.at[4], ydev[LEFT]),
            remote(hop.at[1], into.at[at(2), high], ss.at[5], rr.at[5], ydev[RIGHT]),
        ]
        return first, direct, second

    def y_start(copies):
        first, direct, _ = copies
        for copy in first + direct:
            copy.start()

    def y_relay(copies):
        first, _, second = copies
        for a, b in zip(first, second):
            a.wait_recv()
            b.start()

    def y_wait(copies):
        _, direct, second = copies
        for copy in direct + second:
            copy.wait_recv()

    def y_sent(copies):
        for part in copies:
            for copy in part:
                copy.wait_send()

    def experts(s, g):
        tile = tile_of(width)
        hid[...] = jnp.zeros_like(hid)

        def upper(j, carry):
            cols = pl.ds(pl.multiple_of(j * tile, 128), tile)
            hid[...] += jnp.dot(inc[s, g, :, cols], up[cols, :], preferred_element_type=jnp.float32)
            return carry

        lax.fori_loop(0, width // tile, upper, 0)
        act[...] = jax.nn.silu(hid[...]).astype(jnp.bfloat16)

        def lower(j, carry):
            cols = pl.ds(pl.multiple_of(j * tile, 128), tile)
            out = jnp.dot(act[...], down[:, cols], preferred_element_type=jnp.float32)
            out = out.astype(jnp.bfloat16)
            ret[s, g, 0:rows, cols] = out[0:rows]
            inc[s, g, rows:, cols] = out[rows:]
            return carry

        lax.fori_loop(0, width // tile, lower, 0)

    def rs_copy(s, way, step, c):
        cols = pl.ds(pl.multiple_of(c * quarter, 128), quarter)
        if step == 0:
            source = stage.at[s, :, cols]
        else:
            source = ag.at[s, 4 * way + step - 1, :, cols]
        return remote(
            source, ag.at[s, 4 * way + step, :, cols],
            rs_send.at[s, way, step, c], rs_recv.at[s, way, step, c], zdev[way],
        )

    def share(s, pos, c):
        cols = pl.ds(pl.multiple_of(c * quarter, 128), quarter)
        return jnp.dot(
            gmat[s, pos], ret[s, pos // GROUP, :, cols], preferred_element_type=jnp.float32
        )

    def rs_pos(way, step):
        away = 4 - step
        if away == 4:
            return POS[4]
        return POS[-away if way == LEFT else away]

    def rs_begin(s):
        def body(j, carry):
            for way, c in ((LEFT, j), (RIGHT, j + 2)):
                cols = pl.ds(pl.multiple_of(c * quarter, 128), quarter)
                stage[s, :, cols] = share(s, rs_pos(way, 0), c).astype(jnp.bfloat16)
                rs_copy(s, way, 0, c).start()
            return carry

        lax.fori_loop(0, 2, body, 0)

        def fresh(j, carry):
            for way, c in ((LEFT, j + 2), (RIGHT, j)):
                cols = pl.ds(pl.multiple_of(c * quarter, 128), quarter)
                ag[s, 4 * way, :, cols] = share(s, rs_pos(way, 1), c).astype(jnp.bfloat16)
                rs_copy(s, way, 1, c).start()
            return carry

        lax.fori_loop(0, 2, fresh, 0)

    def rs_add(s, way, step, c):
        cols = pl.ds(pl.multiple_of(c * quarter, 128), quarter)
        own = share(s, rs_pos(way, step), c)
        rs_copy(s, way, step - 1, c).wait_recv()
        total = own + ag[s, 4 * way + step - 1, :, cols].astype(jnp.float32)
        ag[s, 4 * way + step - 1, :, cols] = total.astype(jnp.bfloat16)
        rs_copy(s, way, step, c).start()

    def rs_step(s, step):
        def body(j, carry):
            rs_add(s, LEFT, step, (j + 2) % 4 if step > 1 else j)
            rs_add(s, RIGHT, step, j if step > 1 else j + 2)
            return carry

        lax.fori_loop(0, 4 if step > 1 else 2, body, 0)

    def sh_copy(s, c):
        cols = pl.ds(pl.multiple_of(c * quarter, 128), quarter)
        return remote(
            stage.at[s, :, cols], outs[s].at[:, cols], sh_send.at[s, c], sh_recv.at[s, c], pdev[s]
        )

    def rs_end(s):
        def sent(j, carry):
            rs_copy(s, LEFT, 0, j).wait_send()
            rs_copy(s, RIGHT, 0, j + 2).wait_send()
            return carry

        lax.fori_loop(0, 2, sent, 0)

        def body(j, carry):
            c = (j + 2) % 4
            cols = pl.ds(pl.multiple_of(c * quarter, 128), quarter)
            own = share(s, POS[0], c) + xs[s, :, cols].astype(jnp.float32)
            rs_copy(s, LEFT, 3, c).wait_recv()
            rs_copy(s, RIGHT, 3, c).wait_recv()
            total = own + (
                ag[s, 3, :, cols].astype(jnp.float32) + ag[s, 7, :, cols].astype(jnp.float32)
            )
            stage[s, :, cols] = total.astype(jnp.bfloat16)
            sh_copy(s, c).start()
            return carry

        lax.fori_loop(0, 4, body, 0)

    def rs_sent(s):
        def body(c, carry):
            for way in (LEFT, RIGHT):
                for step in (1, 2, 3):
                    rs_copy(s, way, step, c).wait_send()
            sh_copy(s, c).wait()
            return carry

        lax.fori_loop(0, 4, body, 0)

    def give_credit(s):
        gather_sent(s)
        for way in (LEFT, RIGHT):
            pl.semaphore_signal(credit.at[s], inc=1, device_id=zdev[way], device_id_type=MESH)

    infos[0] = info_ref[...]
    loads[0].wait()
    normalise(0)
    pl.semaphore_wait(barrier, 6)

    gather_hop(0, 1)
    loads[1].wait()
    normalise(1)
    gather_hop(0, 2)
    gather_hop(0, 3)
    select(0, 0)
    y_start(yd_copies(0, 0))
    y_relay(yd_copies(0, 0))
    gather_hop(0, 4)
    gather_hop(1, 1)
    loads[2].wait()
    loads[3].wait()
    y_wait(yd_copies(0, 0))
    experts(0, 0)
    y_start(yr_copies(0, 0))
    gather_end(0)
    select(0, 1)
    y_start(yd_copies(0, 1))
    y_relay(yr_copies(0, 0))
    gather_hop(1, 2)
    give_credit(0)
    y_relay(yd_copies(0, 1))
    y_wait(yd_copies(0, 1))
    experts(0, 1)
    y_start(yr_copies(0, 1))
    gather_hop(1, 3)
    select(1, 0)
    y_start(yd_copies(1, 0))
    y_relay(yr_copies(0, 1))
    y_relay(yd_copies(1, 0))
    y_wait(yr_copies(0, 0))
    y_wait(yr_copies(0, 1))
    gather_hop(1, 4)
    pl.semaphore_wait(credit.at[0], 2)
    rs_begin(0)
    y_wait(yd_copies(1, 0))
    experts(1, 0)
    y_start(yr_copies(1, 0))
    gather_end(1)
    select(1, 1)
    y_start(yd_copies(1, 1))
    rs_step(0, 1)
    give_credit(1)
    y_relay(yr_copies(1, 0))
    y_relay(yd_copies(1, 1))
    rs_step(0, 2)
    y_wait(yd_copies(1, 1))
    experts(1, 1)
    y_start(yr_copies(1, 1))
    rs_step(0, 3)
    y_relay(yr_copies(1, 1))
    y_wait(yr_copies(1, 0))
    y_wait(yr_copies(1, 1))
    pl.semaphore_wait(credit.at[1], 2)
    rs_begin(1)
    rs_end(0)
    rs_step(1, 1)
    rs_step(1, 2)
    rs_step(1, 3)
    rs_end(1)
    for s in (0, 1):
        for g in (0, 1):
            y_sent(yd_copies(s, g))
            y_sent(yr_copies(s, g))
        rs_sent(s)


def shards(stream_fwd, stream_rev, norm_gain, w_up, w_down, routes, gates):
    xf, xr = stream_fwd[0], stream_rev[0]
    upper, lower = w_up[0, 0], w_down[0, 0]
    tok, width = xf.shape
    hidden = upper.shape[1]
    experts = lax.axis_size("expert") // SPLIT
    cap = SPLIT * max(1, tok * TOPK * 5 // (4 * SPLIT * experts))
    picks = routes[0].reshape(2, tok * TOPK)
    match = (picks[:, :, None] == jnp.arange(experts, dtype=jnp.int32)).astype(jnp.bfloat16)
    earlier = jnp.tri(tok * TOPK, k=-1, dtype=jnp.bfloat16)
    before = jnp.einsum("uv,sve->sue", earlier, match, preferred_element_type=jnp.float32)
    slots = jnp.sum(before * match.astype(jnp.float32), axis=-1)
    target = picks.astype(jnp.float32) * cap + slots
    info = jnp.concatenate(
        [
            target.reshape(2, tok, TOPK).transpose(0, 2, 1),
            gates[0].astype(jnp.float32).transpose(0, 2, 1),
        ],
        axis=1,
    ).reshape(8, tok)
    rows = GROUP * cap
    bf16 = jnp.bfloat16
    dma = pltpu.SemaphoreType.DMA
    anywhere = pl.BlockSpec(memory_space=pl.ANY)
    in_vmem = pl.BlockSpec(memory_space=pltpu.VMEM)
    outf, outr = pl.pallas_call(
        functools.partial(kernel, cap),
        out_shape=(jax.ShapeDtypeStruct((tok, width), bf16),) * 2,
        in_specs=[anywhere, anywhere, in_vmem, anywhere, anywhere, in_vmem],
        out_specs=(anywhere, anywhere),
        scratch_shapes=[
            pltpu.VMEM((2, NZ, tok, width), bf16),
            pltpu.VMEM((2, 2, NY * rows, width), bf16),
            pltpu.VMEM((2, 2, (NY - 1) * rows, width), bf16),
            pltpu.VMEM((2, 2, NY * rows, width), bf16),
            pltpu.VMEM((2, 2, 2, 2, rows, width // 2), bf16),
            pltpu.VMEM((NZ, 8, tok), jnp.float32),
            pltpu.VMEM((2, tok, width), bf16),
            pltpu.VMEM((2, tok, width), bf16),
            pltpu.VMEM((width, hidden), bf16),
            pltpu.VMEM((hidden, width), bf16),
            pltpu.VMEM((NY * rows, hidden), bf16),
            pltpu.VMEM((NY * rows, hidden), jnp.float32),
            pltpu.VMEM((2, NZ, tok, NY * rows), bf16),
            dma((2, 2, 4, 2)), dma((2, 2, 4, 2)),
            dma((2, 4)), dma((2, 4)),
            dma((2, 2, 6)), dma((2, 2, 6)),
            dma((2, 2, 6)), dma((2, 2, 6)),
            dma((2, 2, 4, 4)), dma((2, 2, 4, 4)),
            dma((2, 4)), dma((2, 4)),
            dma((4,)),
            pltpu.SemaphoreType.REGULAR((2,)),
        ],
        compiler_params=pltpu.CompilerParams(
            collective_id=0, has_side_effects=True, vmem_limit_bytes=62 * 1024 * 1024
        ),
        cost_estimate=pl.CostEstimate(
            flops=2 * 2 * 2 * NZ * NY * cap * width * hidden,
            bytes_accessed=16 * 1024 * 1024,
            transcendentals=0,
        ),
    )(xf, xr, norm_gain, upper, lower, info)
    return outf[None], outr[None]


def solution(mesh):
    return jax.shard_map(
        shards,
        mesh=mesh,
        in_specs=(
            P("pipe", "expert", None),
            P("pipe", "expert", None),
            P("pipe", None),
            P("pipe", "expert", None, None),
            P("pipe", "expert", None, None),
            P("pipe", None, "expert", None),
            P("pipe", None, "expert", None),
        ),
        out_specs=(P("pipe", "expert", None), P("pipe", "expert", None)),
        check_vma=False,
    )
```

time: 575 us -> 358 us (0.62)
  waiting for transfers between devices: 434 us -> 0 us
  Pallas kernels: 0 us -> 349 us
  local copies, waits for them, and re-layouts: 52.3 us -> 5.63 us
  starting transfers between devices: 41.2 us -> 0 us
  matrix products: 30.6 us -> 0.27 us
  other arithmetic: 13.5 us -> 2 us
    all_to_all x4 -> x0, waiting for transfers between devices: 423 us -> none  [the longest x2 215 us: moe_layer(): lax.all_to_all(outgoing, 'expert', split_axis=0, concat_axis=0, tiled=True)]
    pallas_call x0 -> x1, Pallas kernels: none -> 349 us  [shards(): pl.pallas_call(functools.partial(kernel, cap), out_shape=(jax.ShapeDtypeS...]
    all_to_all x4 -> x0, starting transfers between devices: 37.9 us -> none  [the longest x2 21.2 us: moe_layer(): lax.all_to_all(outgoing, 'expert', split_axis=0, concat_axis=0, tiled=True)]
    reshape x6 -> x0, local copies, waits for them, and re-layouts: 33.5 us -> none  [the longest x2 14.5 us: moe_layer(): partial_value.reshape(devices, cap, width)]
    dot_general x8 -> x1, matrix products: 30.6 us -> 0.27 us  [shards(): jnp.einsum('uv,sve->sue', earlier, match, preferred_element_type=jnp.floa...]
    ppermute x2 -> x0, waiting for transfers between devices: 10.3 us -> none  [shifted(): return lax.ppermute(block, axis, route)]
    broadcast_in_dim x3 -> x0, local copies, waits for them, and re-layouts: 9.16 us -> none  [the longest x2 9.16 us: moe_layer(): outgoing = jnp.repeat(buffer.reshape(experts, cap, width), SPLIT, axis=0)]
    convert_element_type x6 -> x1, other arithmetic: 9.41 us -> 0.68 us  [shards(): target = picks.astype(jnp.float32) * cap + slots]
  transfers between devices with their start and end apart: 6 -> 0, of which waited for: 5 -> 0; matrix products, arithmetic and copies ran while one was open for 13% -> 0% of each run, Pallas kernels for 0% -> 0%
where the time goes in v1:
time: 358 us
  Pallas kernels  349 us (97%)
  local copies, waits for them, and re-layouts  5.63 us (2%)
    pallas_call x1, Pallas kernels, shards(): pl.pallas_call(functools.partial(kernel, cap), out_shape=(jax.ShapeDtypeS...  349 us

profile of v1, /device:TPU:1, one launch (start us, length us, event | category | flops | bytes accessed | tf_op | source)
XLA Modules:
  0.0 357.6 jit_solution(1904544720904495009)
XLA Ops:
  0.6 0.7 convert_bitcast_fusion
  1.3 0.7 convert_element_type.16
  2.0 0.1 copy.13
  2.1 0.8 copy.14
  3.0 0.1 eq.15
  3.1 0.3 fusion.1
  3.4 0.1 reduce_sum.12
  3.6 0.1 copy.15
  3.6 0.6 pad_maximum_fusion
  4.3 349.0 %shard_map.86 = (bf16[128,3584]{1,0:T(8,128)(2,1)}, bf16[128,3584]{1,0:T(8,128)(2,1)}) custom-call(bf16[128,3584]{1,0:T(8,128)(2,1)} %bitcast.34, bf16[128,3584]{1,0:T(8,128)(2,1)} %bitcast.35, bf16[1,3584]{1,0:T(2,128)(2,1)} %gain_ref.1, bf16[3584,512]{1,0:T(8,128)(2,1)} %bitcast.32, bf16[512,3584]{1,0:T(8,128)(2,1)} %bitcast.33, f32[8,128]{1,0:T(8,128)} %bitcast.31), custom_call_target="tpu_custom_call" | custom-call | flops 9395240960 | bytes 16777216 | tf_op jit(solution)/shard_map/pallas_call | solution.py:459
  353.2 2.2 copy.18
  355.4 2.2 copy.19
  (2 shorter events, 0.0 us)

commit v2 on v0

v2 whole, which is shorter than its diff:
```python
import functools

import jax
import jax.numpy as jnp
from jax import lax
from jax.experimental import pallas as pl
from jax.experimental.pallas import tpu as pltpu
from jax.sharding import PartitionSpec as P

SPLIT = 2
TOPK = 2
NY = 4
NZ = 8
GROUP = 4
MESH = pl.DeviceIdType.MESH

POS = {0: 0, -1: 1, 1: 2, 2: 3, -2: 4, -3: 5, 3: 6, 4: 7}
LEFT, RIGHT = 0, 1


def tile_of(width, most=512):
    tile = 128
    for t in range(128, most + 1, 128):
        if width % t == 0:
            tile = t
    return tile


def kernel(
    cap,
    xf_hbm, xr_hbm, gain_ref, up_hbm, down_hbm, info_ref,
    outf_ref, outr_ref,
    ag, inc, sel, ret, infos, xs, stage, up, down, act, hid, gmat,
    ag_send, ag_recv, inf_send, inf_recv, yd_send, yd_recv, yr_send, yr_recv,
    rs_send, rs_recv, sh_send, sh_recv, load_sem, credit,
):
    tok, width = xs.shape[1], xs.shape[2]
    half = width // 2
    quarter = width // 4
    rows = GROUP * cap
    experts = NY * (NZ // SPLIT)
    p = lax.axis_index("pipe")
    e = lax.axis_index("expert")
    n_pipe = lax.axis_size("pipe")
    y, z = e // NZ, e % NZ
    m = z // SPLIT
    zdev = {RIGHT: (p, y * NZ + (z + 1) % NZ), LEFT: (p, y * NZ + (z + NZ - 1) % NZ)}
    ydev = {d: (p, ((y + d) % NY) * NZ + z) for d in (1, 2, 3)}
    pdev = {0: ((p + 1) % n_pipe, e), 1: ((p + n_pipe - 1) % n_pipe, e)}
    outs = {0: outf_ref, 1: outr_ref}

    def remote(src, dst, send, recv, device):
        return pltpu.make_async_remote_copy(
            src_ref=src, dst_ref=dst, send_sem=send, recv_sem=recv,
            device_id=device, device_id_type=MESH,
        )

    barrier = pltpu.get_barrier_semaphore()
    peers = [zdev[0], zdev[1], ydev[1], ydev[2], ydev[3], pdev[0], pdev[1]]
    for device in peers:
        pl.semaphore_signal(barrier, inc=1, device_id=device, device_id_type=MESH)

    load_xf = pltpu.make_async_copy(xf_hbm, xs.at[0], load_sem.at[0])
    load_xr = pltpu.make_async_copy(xr_hbm, xs.at[1], load_sem.at[1])
    load_up = pltpu.make_async_copy(up_hbm, up, load_sem.at[2])
    load_down = pltpu.make_async_copy(down_hbm, down, load_sem.at[3])

    def normalise(s):
        gain = gain_ref[...].astype(jnp.float32)

        def body(i, carry):
            at = pl.ds(pl.multiple_of(i * 16, 16), 16)
            x = xs[s, at, :].astype(jnp.float32)
            scale = lax.rsqrt(jnp.mean(x * x, axis=-1, keepdims=True) + 1e-06)
            ag[s, 0, at, :] = (x * scale * gain).astype(jnp.bfloat16)
            return carry

        lax.fori_loop(0, tok // 16, body, 0)

    def own_info():
        here = lax.broadcasted_iota(jnp.int32, (experts, tok), 0).astype(jnp.float32)
        t0 = lax.broadcasted_iota(jnp.int32, (tok, tok), 0)
        t1 = lax.broadcasted_iota(jnp.int32, (tok, tok), 1)
        earlier = jnp.where(t0 < t1, 1.0, 0.0).astype(jnp.bfloat16)
        for s in (0, 1):
            hits = [here == info_ref[4 * s + k : 4 * s + k + 1, :] for k in range(TOPK)]
            named = jnp.where(hits[0] | hits[1], 1.0, 0.0).astype(jnp.bfloat16)
            before = jnp.dot(named, earlier, preferred_element_type=jnp.float32)
            for k in range(TOPK):
                code = jnp.where(hits[k], here * cap + before, 0.0)
                infos[0, 4 * s + k : 4 * s + k + 1, :] = jnp.sum(code, axis=0, keepdims=True)
            infos[0, 4 * s + 2 : 4 * s + 4, :] = info_ref[4 * s + 2 : 4 * s + 4, :]

    def pos_of(delta):
        return POS[4 if abs(delta) == 4 else delta]

    def ag_copy(s, way, hop, c):
        sign = -1 if way == RIGHT else 1
        cols = pl.ds(c * quarter, quarter)
        return remote(
            ag.at[s, pos_of(sign * (hop - 1)), :, cols], ag.at[s, pos_of(sign * hop), :, cols],
            ag_send.at[s, way, hop - 1, c], ag_recv.at[s, way, hop - 1, c], zdev[way],
        )

    def inf_copy(way, hop):
        sign = -1 if way == RIGHT else 1
        return remote(
            infos.at[pos_of(sign * (hop - 1))], infos.at[pos_of(sign * hop)],
            inf_send.at[way, hop - 1], inf_recv.at[way, hop - 1], zdev[way],
        )

    def inf_ways(hop):
        return (RIGHT, LEFT) if hop < 4 else (RIGHT,)

    def inf_hop(hop):
        for way in inf_ways(hop):
            if hop > 1:
                inf_copy(way, hop - 1).wait_recv()
            inf_copy(way, hop).start()

    def first_chunk(way, h):
        return 2 * h if way == RIGHT else 2 * h + 1

    def gather_hop(s, h, hop):
        for turn in (0, 1):
            for way in (RIGHT, LEFT):
                c = first_chunk(way, h) ^ turn
                if hop > 1:
                    ag_copy(s, way, hop - 1, c).wait_recv()
                ag_copy(s, way, hop, c).start()

    def gather_last(s, h):
        for way in (RIGHT, LEFT):
            c = first_chunk(way, h)
            ag_copy(s, way, 3, c).wait_recv()
            ag_copy(s, way, 4, c).start()

    def gather_end(s, h):
        for way in (RIGHT, LEFT):
            ag_copy(s, way, 3, first_chunk(way, h) ^ 1).wait_recv()
        for way in (RIGHT, LEFT):
            ag_copy(s, way, 4, first_chunk(way, h)).wait_recv()

    def gather_sent(s):
        for h in (0, 1):
            for way in (RIGHT, LEFT):
                for hop in (1, 2, 3):
                    for c in (2 * h, 2 * h + 1):
                        ag_copy(s, way, hop, c).wait_send()
                ag_copy(s, way, 4, first_chunk(way, h)).wait_send()

    def row_codes(shape):
        r = lax.broadcasted_iota(jnp.int32, shape, 0)
        one, zero = jnp.int32(1), jnp.int32(0)
        d = sum(jnp.where(r >= k * rows, one, zero) for k in (1, 2, 3))
        r = r - d * rows
        i = sum(jnp.where(r >= k * cap, one, zero) for k in (1, 2, 3))
        c = r - i * cap
        yd = y + d
        yd = yd - jnp.where(yd >= NY, NY * one, zero)
        expert = yd * (NZ // SPLIT) + m
        return ((i * experts + expert) * cap + c).astype(jnp.float32)

    def select(s, h, g):
        codes = row_codes((NY * rows, tok))
        parts = []
        for i in range(GROUP):
            info = infos[GROUP * g + i]
            shift = float(i * experts * cap)
            hit0 = codes == info[4 * s : 4 * s + 1, :] + shift
            hit1 = codes == info[4 * s + 1 : 4 * s + 2, :] + shift
            parts.append(jnp.where(hit0 | hit1, 1.0, 0.0).astype(jnp.bfloat16))
            if h == 0:
                weights = jnp.where(hit0, info[4 * s + 2 : 4 * s + 3, :], 0.0) + jnp.where(
                    hit1, info[4 * s + 3 : 4 * s + 4, :], 0.0
                )
                gmat[s, GROUP * g + i] = weights.T.astype(jnp.bfloat16)
        pick = jnp.concatenate(parts, axis=1)
        tile = tile_of(half)

        def body(j, carry):
            cols = pl.ds(pl.multiple_of(h * half + j * tile, 128), tile)
            block = ag[s, GROUP * g : GROUP * (g + 1), :, cols].reshape(GROUP * tok, tile)
            out = jnp.dot(pick, block, preferred_element_type=jnp.float32).astype(jnp.bfloat16)
            inc[s, g, 0:rows, cols] = out[0:rows]
            sel[s, g, :, cols] = out[rows:]
            return carry

        lax.fori_loop(0, half // tile, body, 0)
        for d in (1, 2, 3):
            yd_copy(s, h, g, d).start()

    def yd_copy(s, h, g, d):
        cols = pl.ds(h * half, half)
        return remote(
            sel.at[s, g, pl.ds((d - 1) * rows, rows), cols],
            inc.at[s, g, pl.ds(d * rows, rows), cols],
            yd_send.at[s, h, g, d - 1], yd_recv.at[s, h, g, d - 1], ydev[d],
        )

    def yr_copy(s, h, g, d):
        cols = pl.ds(h * half, half)
        block = pl.ds(d * rows, rows)
        return remote(
            inc.at[s, g, block, cols], ret.at[s, g, block, cols],
            yr_send.at[s, h, g, d - 1], yr_recv.at[s, h, g, d - 1], ydev[NY - d],
        )

    def back(s, h, g):
        for d in (1, 2, 3):
            yr_copy(s, h, g, d).wait_recv()

    def upper(s, h, g):
        for d in (1, 2, 3):
            yd_copy(s, h, g, d).wait_recv()
        tile = tile_of(half)
        if h == 0:
            hid[g] = jnp.zeros(hid.shape[1:], jnp.float32)

        def body(j, carry):
            cols = pl.ds(pl.multiple_of(h * half + j * tile, 128), tile)
            hid[g] += jnp.dot(inc[s, g, :, cols], up[cols, :], preferred_element_type=jnp.float32)
            return carry

        lax.fori_loop(0, half // tile, body, 0)
        if h == 1:
            act[g] = jax.nn.silu(hid[g]).astype(jnp.bfloat16)

    def lower(s, h, g):
        tile = tile_of(half)

        def body(j, carry):
            cols = pl.ds(pl.multiple_of(h * half + j * tile, 128), tile)
            out = jnp.dot(act[g], down[:, cols], preferred_element_type=jnp.float32)
            out = out.astype(jnp.bfloat16)
            ret[s, g, 0:rows, cols] = out[0:rows]
            inc[s, g, rows:, cols] = out[rows:]
            return carry

        lax.fori_loop(0, half // tile, body, 0)
        for d in (2, 1, 3):
            yr_copy(s, h, g, d).start()

    def rs_copy(s, way, step, c):
        cols = pl.ds(c * quarter, quarter)
        if step == 0:
            source = stage.at[s, :, cols]
        else:
            source = ag.at[s, 4 * way + step - 1, :, cols]
        return remote(
            source, ag.at[s, 4 * way + step, :, cols],
            rs_send.at[s, way, step, c], rs_recv.at[s, way, step, c], zdev[way],
        )

    def share(s, pos, c):
        cols = pl.ds(c * quarter, quarter)
        return jnp.dot(
            gmat[s, pos], ret[s, pos // GROUP, :, cols], preferred_element_type=jnp.float32
        )

    def rs_pos(way, step):
        away = 4 - step
        if away == 4:
            return POS[4]
        return POS[-away if way == LEFT else away]

    def rs_first(way, h):
        return 2 * h if way == LEFT else 2 * h + 1

    def rs_begin(s, h):
        for way in (LEFT, RIGHT):
            c = rs_first(way, h)
            stage[s, :, pl.ds(c * quarter, quarter)] = share(s, rs_pos(way, 0), c).astype(jnp.bfloat16)
            rs_copy(s, way, 0, c).start()
        for way in (LEFT, RIGHT):
            c = rs_first(way, h) ^ 1
            ag[s, 4 * way, :, pl.ds(c * quarter, quarter)] = share(s, rs_pos(way, 1), c).astype(
                jnp.bfloat16
            )
            rs_copy(s, way, 1, c).start()

    def rs_add(s, way, step, c):
        cols = pl.ds(c * quarter, quarter)
        own = share(s, rs_pos(way, step), c)
        rs_copy(s, way, step - 1, c).wait_recv()
        total = own + ag[s, 4 * way + step - 1, :, cols].astype(jnp.float32)
        ag[s, 4 * way + step - 1, :, cols] = total.astype(jnp.bfloat16)
        rs_copy(s, way, step, c).start()

    def rs_step(s, h, step):
        for turn in (1, 0) if step > 1 else (0,):
            for way in (LEFT, RIGHT):
                rs_add(s, way, step, rs_first(way, h) ^ turn)

    def sh_copy(s, c):
        cols = pl.ds(c * quarter, quarter)
        return remote(
            stage.at[s, :, cols], outs[s].at[:, cols], sh_send.at[s, c], sh_recv.at[s, c], pdev[s]
        )

    def rs_end(s, h):
        for way in (LEFT, RIGHT):
            rs_copy(s, way, 0, rs_first(way, h)).wait_send()
        for c in (2 * h, 2 * h + 1):
            cols = pl.ds(c * quarter, quarter)
            own = share(s, POS[0], c) + xs[s, :, cols].astype(jnp.float32)
            rs_copy(s, LEFT, 3, c).wait_recv()
            rs_copy(s, RIGHT, 3, c).wait_recv()
            total = own + (
                ag[s, 3, :, cols].astype(jnp.float32) + ag[s, 7, :, cols].astype(jnp.float32)
            )
            stage[s, :, cols] = total.astype(jnp.bfloat16)
            sh_copy(s, c).start()

    def finish(s):
        for h in (0, 1):
            for g in (0, 1):
                for d in (1, 2, 3):
                    yd_copy(s, h, g, d).wait_send()
                    yr_copy(s, h, g, d).wait_send()
            for c in (2 * h, 2 * h + 1):
                for way in (LEFT, RIGHT):
                    for step in (1, 2, 3):
                        rs_copy(s, way, step, c).wait_send()
                sh_copy(s, c).wait()

    def give_credit(s):
        gather_sent(s)
        for way in (LEFT, RIGHT):
            pl.semaphore_signal(credit.at[s], inc=1, device_id=zdev[way], device_id_type=MESH)

    f, r, near, far = 0, 1, 0, 1

    load_xf.start()
    load_xr.start()
    own_info()
    load_xf.wait()
    normalise(f)
    pl.semaphore_wait(barrier, len(peers))

    inf_hop(1)
    gather_hop(f, 0, 1)
    load_up.start()
    load_down.start()
    load_xr.wait()
    normalise(r)
    inf_hop(2)
    gather_hop(f, 0, 2)
    inf_hop(3)
    gather_hop(f, 0, 3)
    select(f, 0, near)
    inf_hop(4)
    gather_last(f, 0)
    gather_hop(f, 1, 1)
    load_up.wait()
    load_down.wait()
    inf_copy(RIGHT, 4).wait_recv()
    inf_copy(LEFT, 3).wait_recv()
    gather_end(f, 0)
    select(f, 0, far)
    gather_hop(f, 1, 2)
    upper(f, 0, near)
    gather_hop(f, 1, 3)
    select(f, 1, near)
    upper(f, 0, far)
    gather_last(f, 1)
    gather_hop(r, 0, 1)
    gather_end(f, 1)
    select(f, 1, far)
    gather_hop(r, 0, 2)
    upper(f, 1, near)
    give_credit(f)
    gather_hop(r, 0, 3)
    select(r, 0, near)
    upper(f, 1, far)
    lower(f, 0, far)
    gather_last(r, 0)
    gather_hop(r, 1, 1)
    lower(f, 0, near)
    gather_end(r, 0)
    select(r, 0, far)
    gather_hop(r, 1, 2)
    upper(r, 0, near)
    lower(f, 1, far)
    gather_hop(r, 1, 3)
    select(r, 1, near)
    gather_last(r, 1)
    back(f, 0, far)
    pl.semaphore_wait(credit.at[f], 2)
    rs_begin(f, 0)
    gather_end(r, 1)
    select(r, 1, far)
    back(f, 0, near)
    rs_step(f, 0, 1)
    give_credit(r)
    rs_step(f, 0, 2)
    upper(r, 0, far)
    lower(f, 1, near)
    rs_step(f, 0, 3)
    back(f, 1, far)
    rs_begin(f, 1)
    rs_end(f, 0)
    upper(r, 1, near)
    rs_step(f, 1, 1)
    back(f, 1, near)
    rs_step(f, 1, 2)
    upper(r, 1, far)
    lower(r, 0, far)
    lower(r, 0, near)
    rs_step(f, 1, 3)
    lower(r, 1, far)
    lower(r, 1, near)
    pl.semaphore_wait(credit.at[r], 2)
    back(r, 0, far)
    rs_begin(r, 0)
    rs_end(f, 1)
    rs_step(r, 0, 1)
    back(r, 0, near)
    rs_step(r, 0, 2)
    rs_step(r, 0, 3)
    back(r, 1, far)
    rs_begin(r, 1)
    rs_end(r, 0)
    rs_step(r, 1, 1)
    back(r, 1, near)
    rs_step(r, 1, 2)
    rs_step(r, 1, 3)
    rs_end(r, 1)
    for hop in (1, 2, 3, 4):
        for way in inf_ways(hop):
            inf_copy(way, hop).wait_send()
    finish(f)
    finish(r)


def shards(stream_fwd, stream_rev, norm_gain, w_up, w_down, routes, gates):
    xf, xr = stream_fwd[0], stream_rev[0]
    upper, lower = w_up[0, 0], w_down[0, 0]
    tok, width = xf.shape
    hidden = upper.shape[1]
    experts = lax.axis_size("expert") // SPLIT
    cap = SPLIT * max(1, tok * TOPK * 5 // (4 * SPLIT * experts))
    info = jnp.concatenate([routes[0].astype(jnp.float32), gates[0].astype(jnp.float32)], axis=-1)
    info = info.transpose(0, 2, 1).reshape(8, tok)
    rows = GROUP * cap
    bf16 = jnp.bfloat16
    dma = pltpu.SemaphoreType.DMA
    anywhere = pl.BlockSpec(memory_space=pl.ANY)
    in_vmem = pl.BlockSpec(memory_space=pltpu.VMEM)
    outf, outr = pl.pallas_call(
        functools.partial(kernel, cap),
        out_shape=(jax.ShapeDtypeStruct((tok, width), bf16),) * 2,
        in_specs=[anywhere, anywhere, in_vmem, anywhere, anywhere, in_vmem],
        out_specs=(anywhere, anywhere),
        scratch_shapes=[
            pltpu.VMEM((2, NZ, tok, width), bf16),
            pltpu.VMEM((2, 2, NY * rows, width), bf16),
            pltpu.VMEM((2, 2, (NY - 1) * rows, width), bf16),
            pltpu.VMEM((2, 2, NY * rows, width), bf16),
            pltpu.VMEM((NZ, 8, tok), jnp.float32),
            pltpu.VMEM((2, tok, width), bf16),
            pltpu.VMEM((2, tok, width), bf16),
            pltpu.VMEM((width, hidden), bf16),
            pltpu.VMEM((hidden, width), bf16),
            pltpu.VMEM((2, NY * rows, hidden), bf16),
            pltpu.VMEM((2, NY * rows, hidden), jnp.float32),
            pltpu.VMEM((2, NZ, tok, NY * rows), bf16),
            dma((2, 2, 4, 4)), dma((2, 2, 4, 4)),
            dma((2, 4)), dma((2, 4)),
            dma((2, 2, 2, 3)), dma((2, 2, 2, 3)),
            dma((2, 2, 2, 3)), dma((2, 2, 2, 3)),
            dma((2, 2, 4, 4)), dma((2, 2, 4, 4)),
            dma((2, 4)), dma((2, 4)),
            dma((4,)),
            pltpu.SemaphoreType.REGULAR((2,)),
        ],
        compiler_params=pltpu.CompilerParams(
            collective_id=0, has_side_effects=True, vmem_limit_bytes=62 * 1024 * 1024
        ),
        cost_estimate=pl.CostEstimate(
            flops=2 * 2 * 2 * NZ * NY * cap * width * hidden,
            bytes_accessed=16 * 1024 * 1024,
            transcendentals=0,
        ),
    )(xf, xr, norm_gain, upper, lower, info)
    return outf[None], outr[None]


def solution(mesh):
    return jax.shard_map(
        shards,
        mesh=mesh,
        in_specs=(
            P("pipe", "expert", None),
            P("pipe", "expert", None),
            P("pipe", None),
            P("pipe", "expert", None, None),
            P("pipe", "expert", None, None),
            P("pipe", None, "expert", None),
            P("pipe", None, "expert", None),
        ),
        out_specs=(P("pipe", "expert", None), P("pipe", "expert", None)),
        check_vma=False,
    )
```

time: 575 us -> 311 us (0.54)
  waiting for transfers between devices: 434 us -> 0 us
  Pallas kernels: 0 us -> 304 us
  local copies, waits for them, and re-layouts: 52.3 us -> 4.32 us
  starting transfers between devices: 41.2 us -> 0 us
  matrix products: 30.6 us -> 0 us
  other arithmetic: 13.5 us -> 1.97 us
    all_to_all x4 -> x0, waiting for transfers between devices: 423 us -> none  [the longest x2 215 us: moe_layer(): lax.all_to_all(outgoing, 'expert', split_axis=0, concat_axis=0, tiled=True)]
    pallas_call x0 -> x1, Pallas kernels: none -> 304 us  [shards(): pl.pallas_call(functools.partial(kernel, cap), out_shape=(jax.ShapeDtypeS...]
    all_to_all x4 -> x0, starting transfers between devices: 37.9 us -> none  [the longest x2 21.2 us: moe_layer(): lax.all_to_all(outgoing, 'expert', split_axis=0, concat_axis=0, tiled=True)]
    reshape x6 -> x0, local copies, waits for them, and re-layouts: 33.5 us -> none  [the longest x2 14.5 us: moe_layer(): partial_value.reshape(devices, cap, width)]
    dot_general x8 -> x0, matrix products: 30.6 us -> none  [the longest x2 12.5 us: expert_rows(): jnp.dot(rows, upper, preferred_element_type=jnp.float32)]
    ppermute x2 -> x0, waiting for transfers between devices: 10.3 us -> none  [shifted(): return lax.ppermute(block, axis, route)]
    broadcast_in_dim x3 -> x0, local copies, waits for them, and re-layouts: 9.16 us -> none  [the longest x2 9.16 us: moe_layer(): outgoing = jnp.repeat(buffer.reshape(experts, cap, width), SPLIT, axis=0)]
    convert_element_type x6 -> x2, other arithmetic: 9.41 us -> 1.37 us  [the longest x1 0.68 us: shards(): routes[0].astype(jnp.float32)]
  transfers between devices with their start and end apart: 6 -> 0, of which waited for: 5 -> 0; matrix products, arithmetic and copies ran while one was open for 13% -> 0% of each run, Pallas kernels for 0% -> 0%
where the time goes in v2:
time: 311 us
  Pallas kernels  304 us (98%)
  local copies, waits for them, and re-layouts  4.32 us (1%)
    pallas_call x1, Pallas kernels, shards(): pl.pallas_call(functools.partial(kernel, cap), out_shape=(jax.ShapeDtypeS...  304 us

profile of v2, /device:TPU:1, one launch (start us, length us, event | category | flops | bytes accessed | tf_op | source)
XLA Modules:
  0.0 310.8 jit_solution(7287158935163252518)
XLA Ops:
  0.6 0.7 convert_bitcast_fusion
  1.3 0.7 bitcast_convert_fusion
  2.0 0.6 pad_maximum_fusion
  2.6 303.9 %shard_map.86 = (bf16[128,3584]{1,0:T(8,128)(2,1)}, bf16[128,3584]{1,0:T(8,128)(2,1)}) custom-call(bf16[128,3584]{1,0:T(8,128)(2,1)} %bitcast.19, bf16[128,3584]{1,0:T(8,128)(2,1)} %bitcast.20, bf16[1,3584]{1,0:T(2,128)(2,1)} %gain_ref.1, bf16[3584,512]{1,0:T(8,128)(2,1)} %bitcast.17, bf16[512,3584]{1,0:T(8,128)(2,1)} %bitcast.18, f32[8,128]{1,0:T(8,128)} %bitcast.16), custom_call_target="tpu_custom_call" | custom-call | flops 9395240960 | bytes 16777216 | tf_op jit(solution)/shard_map/pallas_call | solution.py:450
  306.5 2.2 copy.11
  308.6 2.2 copy.12

commit v3 on v2

v3 whole, which is shorter than its diff:
```python
import functools

import jax
import jax.numpy as jnp
from jax import lax
from jax.experimental import pallas as pl
from jax.experimental.pallas import tpu as pltpu
from jax.sharding import PartitionSpec as P

SPLIT = 2
TOPK = 2
NY = 4
NZ = 8
GROUP = 4
MESH = pl.DeviceIdType.MESH

IN, OUT = 0, 1
NEAR, FAR = 0, 1


def tile_of(width, most=512):
    tile = 128
    for t in range(128, most + 1, 128):
        if width % t == 0:
            tile = t
    return tile


def kernel(
    cap,
    xf_hbm, xr_hbm, gain_ref, up_hbm, down_hbm, info_ref,
    outf_ref, outr_ref,
    ag, pkd, stag, tmp, inc, sel, ret, infos, xs, stage, up, down, act, hid,
    gmat, order, leaf, pack, spread,
    ag_send, ag_recv, inf_send, inf_recv, yd_send, yd_recv, yr_send, yr_recv,
    rs_send, rs_recv, sh_send, sh_recv, load_sem, credit,
):
    tok, width = xs.shape[1], xs.shape[2]
    half = width // 2
    quarter = width // 4
    rows = GROUP * cap
    slots = NY * cap
    per_y = NZ // SPLIT
    experts = NY * per_y
    p = lax.axis_index("pipe")
    e = lax.axis_index("expert")
    n_pipe = lax.axis_size("pipe")
    y, z = e // NZ, e % NZ
    odd = z % 2
    z_in = z + 1 - 2 * odd
    z_out = (z + NZ - 1 + 2 * odd) % NZ
    zdev = {IN: (p, y * NZ + z_in), OUT: (p, y * NZ + z_out)}
    ydev = {d: (p, ((y + d) % NY) * NZ + z) for d in (1, 2, 3)}
    pdev = {0: ((p + 1) % n_pipe, e), 1: ((p + n_pipe - 1) % n_pipe, e)}
    outs = {0: outf_ref, 1: outr_ref}

    def remote(src, dst, send, recv, device):
        return pltpu.make_async_remote_copy(
            src_ref=src, dst_ref=dst, send_sem=send, recv_sem=recv,
            device_id=device, device_id_type=MESH,
        )

    def chunk(c):
        return pl.ds(c * quarter, quarter)

    barrier = pltpu.get_barrier_semaphore()
    peers = [zdev[0], zdev[1], ydev[1], ydev[2], ydev[3], pdev[0], pdev[1]]
    for device in peers:
        pl.semaphore_signal(barrier, inc=1, device_id=device, device_id_type=MESH)

    load_xf = pltpu.make_async_copy(xf_hbm, xs.at[0], load_sem.at[0])
    load_xr = pltpu.make_async_copy(xr_hbm, xs.at[1], load_sem.at[1])
    load_up = pltpu.make_async_copy(up_hbm, up, load_sem.at[2])
    load_down = pltpu.make_async_copy(down_hbm, down, load_sem.at[3])

    def normalise(s):
        gain = gain_ref[...].astype(jnp.float32)

        def body(i, carry):
            at = pl.ds(pl.multiple_of(i * 16, 16), 16)
            x = xs[s, at, :].astype(jnp.float32)
            scale = lax.rsqrt(jnp.mean(x * x, axis=-1, keepdims=True) + 1e-06)
            ag[s, 0, at, :] = (x * scale * gain).astype(jnp.bfloat16)
            return carry

        lax.fori_loop(0, tok // 16, body, 0)

    def own_info():
        here = lax.broadcasted_iota(jnp.int32, (experts, tok), 0).astype(jnp.float32)
        t0 = lax.broadcasted_iota(jnp.int32, (tok, tok), 0)
        t1 = lax.broadcasted_iota(jnp.int32, (tok, tok), 1)
        earlier = jnp.where(t0 < t1, 1.0, 0.0).astype(jnp.bfloat16)
        for s in (0, 1):
            hits = [here == info_ref[4 * s + k : 4 * s + k + 1, :] for k in range(TOPK)]
            named = jnp.where(hits[0] | hits[1], 1.0, 0.0).astype(jnp.bfloat16)
            before = jnp.dot(named, earlier, preferred_element_type=jnp.float32)
            for k in range(TOPK):
                code = jnp.where(hits[k], here * cap + before, 0.0)
                infos[0, 4 * s + k : 4 * s + k + 1, :] = jnp.sum(code, axis=0, keepdims=True)
            infos[0, 4 * s + 2 : 4 * s + 4, :] = info_ref[4 * s + 2 : 4 * s + 4, :]

    def ag_copy(s, way, hop, c):
        if way == IN:
            buf, src, dst = {
                1: (ag, ag.at[s, 0], 2), 2: (ag, ag.at[s, 1], 3),
                3: (pkd, pkd.at[s, 0], 2), 4: (pkd, pkd.at[s, 1], 3),
            }[hop]
        else:
            buf, src, dst = {
                1: (ag, ag.at[s, 0], 1), 2: (pkd, stag.at[s, 0], 0), 3: (pkd, stag.at[s, 1], 1),
            }[hop]
        return remote(
            src.at[:, chunk(c)], buf.at[s, dst, :, chunk(c)],
            ag_send.at[s, way, hop - 1, c], ag_recv.at[s, way, hop - 1, c], zdev[way],
        )

    INFO = ((IN, 0, 2), (OUT, 0, 1), (IN, 1, 3))

    def inf_copy(i):
        way, source, target = INFO[i]
        return remote(infos.at[source], infos.at[target], inf_send.at[i], inf_recv.at[i], zdev[way])

    def chunks(h):
        return (2 * h, 2 * h + 1)

    def own_send(s, h, ways):
        for c in chunks(h):
            for way in ways:
                ag_copy(s, way, 1, c).start()

    def pack_send(s, far, c):
        block = jnp.dot(pack[s, far], ag[s, 2 + far, :, chunk(c)], preferred_element_type=jnp.float32)
        stag[s, far, :, chunk(c)] = block.astype(jnp.bfloat16)
        ag_copy(s, OUT, 2 + far, c).start()

    def second_hop(s, h):
        for c in chunks(h):
            ag_copy(s, OUT, 1, c).wait_recv()
            ag_copy(s, IN, 2, c).start()
            ag_copy(s, IN, 1, c).wait_recv()
            pack_send(s, 0, c)

    def third_hop(s, h):
        for c in chunks(h):
            ag_copy(s, OUT, 2, c).wait_recv()
            ag_copy(s, IN, 3, c).start()
            ag_copy(s, IN, 2, c).wait_recv()
            pack_send(s, 1, c)

    def fourth_hop(s, h):
        for c in chunks(h):
            ag_copy(s, OUT, 3, c).wait_recv()
            ag_copy(s, IN, 4, c).start()

    def gather_end(s, h):
        for hop in (3, 4):
            for c in chunks(h):
                ag_copy(s, IN, hop, c).wait_recv()

    def gather_sent(s):
        for c in range(4):
            for hop in (1, 2, 3, 4):
                ag_copy(s, IN, hop, c).wait_send()
            for hop in (1, 2, 3):
                ag_copy(s, OUT, hop, c).wait_send()

    def split_rows(shape):
        r = lax.broadcasted_iota(jnp.int32, shape, 0)
        one, zero = jnp.int32(1), jnp.int32(0)
        u = sum(jnp.where(r >= k * rows, one, zero) for k in (1, 2, 3))
        r = r - u * rows
        v = sum(jnp.where(r >= k * cap, one, zero) for k in (1, 2, 3))
        return u, v, r - v * cap

    def expert_at(d, pair):
        yd = y + d
        yd = yd - jnp.where(yd >= NY, jnp.int32(NY), jnp.int32(0))
        return yd * per_y + pair

    def constants():
        d, i, c = split_rows((NY * rows, NY * rows))
        column = lax.broadcasted_iota(jnp.int32, (NY * rows, NY * rows), 1)
        order[...] = jnp.where(column == i * slots + d * cap + c, 1.0, 0.0).astype(jnp.bfloat16)
        _, d, c = split_rows((slots, NY * rows))
        column = lax.broadcasted_iota(jnp.int32, (slots, NY * rows), 1)
        for i in range(GROUP):
            leaf[i] = jnp.where(column == d * rows + i * cap + c, 1.0, 0.0).astype(jnp.bfloat16)

    def hits_of(s, info, codes):
        hit0 = codes == info[4 * s : 4 * s + 1, :]
        hit1 = codes == info[4 * s + 1 : 4 * s + 2, :]
        weights = jnp.where(hit0, info[4 * s + 2 : 4 * s + 3, :], 0.0) + jnp.where(
            hit1, info[4 * s + 3 : 4 * s + 4, :], 0.0
        )
        return jnp.where(hit0 | hit1, 1.0, 0.0).astype(jnp.bfloat16), weights.T.astype(jnp.bfloat16)

    def pack_matrices(far):
        _, d, c = split_rows((slots, tok))
        codes = (expert_at(d, z_out // SPLIT) * cap + c).astype(jnp.float32)
        info = infos[2 + far]
        for s in (0, 1):
            pack[s, far], spread[s, far] = hits_of(s, info, codes)

    def select(s, h, g):
        if g == NEAR:
            d, at, c = split_rows((NY * rows, tok))
            codes = (expert_at(d, z // SPLIT) * cap + c).astype(jnp.float32)
            parts = []
            for i in range(GROUP):
                mine, weights = hits_of(s, infos[i], jnp.where(at == i, codes, -1.0))
                parts.append(mine)
                if h == 0:
                    gmat[s, i] = weights
            pick = jnp.concatenate(parts, axis=1)
            source, depth = ag, tok
        else:
            pick = order[...]
            source, depth = pkd, slots
        tile = tile_of(half)

        def body(j, carry):
            cols = pl.ds(pl.multiple_of(h * half + j * tile, 128), tile)
            block = source[s, :, :, cols].reshape(GROUP * depth, tile)
            out = jnp.dot(pick, block, preferred_element_type=jnp.float32).astype(jnp.bfloat16)
            inc[s, g, 0:rows, cols] = out[0:rows]
            sel[s, g, :, cols] = out[rows:]
            return carry

        lax.fori_loop(0, half // tile, body, 0)
        for d in (1, 2, 3):
            yd_copy(s, h, g, d).start()

    def yd_copy(s, h, g, d):
        cols = pl.ds(h * half, half)
        return remote(
            sel.at[s, g, pl.ds((d - 1) * rows, rows), cols],
            inc.at[s, g, pl.ds(d * rows, rows), cols],
            yd_send.at[s, h, g, d - 1], yd_recv.at[s, h, g, d - 1], ydev[d],
        )

    def yr_copy(s, h, g, d):
        cols = pl.ds(h * half, half)
        block = pl.ds(d * rows, rows)
        return remote(
            inc.at[s, g, block, cols], ret.at[s, g, block, cols],
            yr_send.at[s, h, g, d - 1], yr_recv.at[s, h, g, d - 1], ydev[NY - d],
        )

    def back(s, h, g):
        for d in (1, 2, 3):
            yr_copy(s, h, g, d).wait_recv()

    def upper(s, h, g):
        for d in (1, 2, 3):
            yd_copy(s, h, g, d).wait_recv()
        tile = tile_of(half)
        if h == 0:
            hid[g] = jnp.zeros(hid.shape[1:], jnp.float32)

        def body(j, carry):
            cols = pl.ds(pl.multiple_of(h * half + j * tile, 128), tile)
            hid[g] += jnp.dot(inc[s, g, :, cols], up[cols, :], preferred_element_type=jnp.float32)
            return carry

        lax.fori_loop(0, half // tile, body, 0)
        if h == 1:
            act[g] = jax.nn.silu(hid[g]).astype(jnp.bfloat16)

    def lower(s, h, g):
        tile = tile_of(half)

        def body(j, carry):
            cols = pl.ds(pl.multiple_of(h * half + j * tile, 128), tile)
            out = jnp.dot(act[g], down[:, cols], preferred_element_type=jnp.float32)
            out = out.astype(jnp.bfloat16)
            ret[s, g, 0:rows, cols] = out[0:rows]
            inc[s, g, rows:, cols] = out[rows:]
            return carry

        lax.fori_loop(0, half // tile, body, 0)
        for d in (2, 1, 3):
            yr_copy(s, h, g, d).start()

    def rs_copy(s, way, step, c):
        if way == IN:
            buf, src, dst = {
                0: (pkd, stag.at[s, 0], 1), 1: (pkd, stag.at[s, 1], 0),
                2: (ag, ag.at[s, 3], 1), 3: (ag, tmp.at[s], 0),
            }[step]
        else:
            buf, src, dst = {
                0: (pkd, pkd.at[s, 1], 2), 1: (pkd, pkd.at[s, 0], 3), 2: (ag, ag.at[s, 1], 2),
            }[step]
        return remote(
            src.at[:, chunk(c)], buf.at[s, dst, :, chunk(c)],
            rs_send.at[s, way, step, c], rs_recv.at[s, way, step, c], zdev[way],
        )

    def near_rows(s, i, c):
        return jnp.dot(gmat[s, i], ret[s, NEAR, :, chunk(c)], preferred_element_type=jnp.float32)

    def far_rows(s, i, c):
        return jnp.dot(leaf[i], ret[s, FAR, :, chunk(c)], preferred_element_type=jnp.float32)

    def rs_begin(s, h):
        for step, i in ((0, 3), (1, 2)):
            for c in chunks(h):
                stag[s, step, :, chunk(c)] = far_rows(s, i, c).astype(jnp.bfloat16)
                rs_copy(s, IN, step, c).start()

    def pair_sum(s, step, c):
        own = far_rows(s, 1 - step, c)
        rs_copy(s, IN, step, c).wait_recv()
        total = own + pkd[s, 1 - step, :, chunk(c)].astype(jnp.float32)
        pkd[s, 1 - step, :, chunk(c)] = total.astype(jnp.bfloat16)
        rs_copy(s, OUT, step, c).start()

    def spread_sum(s, step, c):
        own = near_rows(s, 3 - step, c)
        rs_copy(s, OUT, step, c).wait_recv()
        total = own + jnp.dot(
            spread[s, 1 - step], pkd[s, 2 + step, :, chunk(c)], preferred_element_type=jnp.float32
        )
        if step == 0:
            ag[s, 3, :, chunk(c)] = total.astype(jnp.bfloat16)
        else:
            tmp[s, :, chunk(c)] = total.astype(jnp.bfloat16)
        rs_copy(s, IN, 2 + step, c).start()

    def pass_sum(s, c):
        own = near_rows(s, 1, c)
        rs_copy(s, IN, 2, c).wait_recv()
        total = own + ag[s, 1, :, chunk(c)].astype(jnp.float32)
        ag[s, 1, :, chunk(c)] = total.astype(jnp.bfloat16)
        rs_copy(s, OUT, 2, c).start()

    def rs_mid_a(s, h):
        for c in chunks(h):
            pair_sum(s, 0, c)

    def rs_mid_b(s, h):
        for c in chunks(h):
            spread_sum(s, 0, c)
            pair_sum(s, 1, c)

    def rs_late_a(s, h):
        for c in chunks(h):
            spread_sum(s, 1, c)

    def rs_late_b(s, h):
        for c in chunks(h):
            pass_sum(s, c)

    def sh_copy(s, c):
        return remote(
            stage.at[s, :, chunk(c)], outs[s].at[:, chunk(c)], sh_send.at[s, c], sh_recv.at[s, c], pdev[s]
        )

    def rs_end(s, h):
        for c in chunks(h):
            own = near_rows(s, 0, c) + xs[s, :, chunk(c)].astype(jnp.float32)
            rs_copy(s, OUT, 2, c).wait_recv()
            rs_copy(s, IN, 3, c).wait_recv()
            total = own + (
                ag[s, 0, :, chunk(c)].astype(jnp.float32) + ag[s, 2, :, chunk(c)].astype(jnp.float32)
            )
            stage[s, :, chunk(c)] = total.astype(jnp.bfloat16)
            sh_copy(s, c).start()

    def finish(s):
        for h in (0, 1):
            for g in (0, 1):
                for d in (1, 2, 3):
                    yd_copy(s, h, g, d).wait_send()
                    yr_copy(s, h, g, d).wait_send()
        for c in range(4):
            for step in (0, 1, 2, 3):
                rs_copy(s, IN, step, c).wait_send()
            for step in (0, 1, 2):
                rs_copy(s, OUT, step, c).wait_send()
            sh_copy(s, c).wait()

    def give_credit(s):
        gather_sent(s)
        for way in (IN, OUT):
            pl.semaphore_signal(credit.at[s], inc=1, device_id=zdev[way], device_id_type=MESH)

    f, r, near, far = 0, 1, NEAR, FAR
    both = (IN, OUT)

    load_xf.start()
    load_xr.start()
    own_info()
    load_xf.wait()
    normalise(f)
    pl.semaphore_wait(barrier, len(peers))

    inf_copy(0).start()
    inf_copy(1).start()
    own_send(f, 0, (IN,))
    own_send(f, 0, (OUT,))
    constants()
    load_up.start()
    load_down.start()
    inf_copy(1).wait_recv()
    inf_copy(2).start()
    inf_copy(0).wait_recv()
    pack_matrices(0)
    second_hop(f, 0)
    inf_copy(2).wait_recv()
    pack_matrices(1)
    third_hop(f, 0)
    select(f, 0, near)
    fourth_hop(f, 0)
    own_send(f, 1, (OUT,))
    own_send(f, 1, (IN,))
    load_xr.wait()
    normalise(r)
    gather_end(f, 0)
    select(f, 0, far)
    second_hop(f, 1)
    third_hop(f, 1)
    select(f, 1, near)
    fourth_hop(f, 1)
    load_up.wait()
    load_down.wait()
    upper(f, 0, near)
    own_send(r, 0, (OUT,))
    own_send(r, 1, (OUT,))
    own_send(r, 0, (IN,))
    gather_end(f, 1)
    select(f, 1, far)
    own_send(r, 1, (IN,))
    upper(f, 0, far)
    upper(f, 1, near)
    lower(f, 1, near)
    upper(f, 1, far)
    lower(f, 1, far)
    second_hop(r, 1)
    lower(f, 0, far)
    second_hop(r, 0)
    third_hop(r, 0)
    fourth_hop(r, 0)
    third_hop(r, 1)
    select(r, 0, near)
    fourth_hop(r, 1)
    gather_end(r, 0)
    give_credit(f)
    lower(f, 0, near)
    back(f, 1, far)
    select(r, 0, far)
    back(f, 0, far)
    back(f, 1, near)
    pl.semaphore_wait(credit.at[f], 2)
    rs_begin(f, 0)
    gather_end(r, 1)
    rs_mid_a(f, 0)
    upper(r, 0, near)
    rs_begin(f, 1)
    select(r, 1, far)
    back(f, 0, near)
    rs_mid_a(f, 1)
    rs_mid_b(f, 0)
    rs_mid_b(f, 1)
    select(r, 1, near)
    upper(r, 0, far)
    rs_late_a(f, 1)
    upper(r, 1, far)
    lower(r, 0, far)
    rs_late_b(f, 1)
    upper(r, 1, near)
    give_credit(r)
    rs_late_a(f, 0)
    lower(r, 0, near)
    rs_end(f, 1)
    rs_late_b(f, 0)
    back(r, 0, far)
    pl.semaphore_wait(credit.at[r], 2)
    rs_begin(r, 0)
    rs_mid_a(r, 0)
    lower(r, 1, far)
    back(r, 0, near)
    rs_mid_b(r, 0)
    rs_late_a(r, 0)
    rs_late_b(r, 0)
    lower(r, 1, near)
    back(r, 1, far)
    rs_begin(r, 1)
    rs_mid_a(r, 1)
    rs_end(f, 0)
    back(r, 1, near)
    rs_mid_b(r, 1)
    rs_late_a(r, 1)
    rs_late_b(r, 1)
    rs_end(r, 0)
    rs_end(r, 1)
    for i in range(len(INFO)):
        inf_copy(i).wait_send()
    finish(f)
    finish(r)


def shards(stream_fwd, stream_rev, norm_gain, w_up, w_down, routes, gates):
    xf, xr = stream_fwd[0], stream_rev[0]
    upper, lower = w_up[0, 0], w_down[0, 0]
    tok, width = xf.shape
    hidden = upper.shape[1]
    experts = lax.axis_size("expert") // SPLIT
    cap = SPLIT * max(1, tok * TOPK * 5 // (4 * SPLIT * experts))
    info = jnp.concatenate([routes[0].astype(jnp.float32), gates[0].astype(jnp.float32)], axis=-1)
    info = info.transpose(0, 2, 1).reshape(8, tok)
    rows = GROUP * cap
    bf16 = jnp.bfloat16
    dma = pltpu.SemaphoreType.DMA
    anywhere = pl.BlockSpec(memory_space=pl.ANY)
    in_vmem = pl.BlockSpec(memory_space=pltpu.VMEM)
    outf, outr = pl.pallas_call(
        functools.partial(kernel, cap),
        out_shape=(jax.ShapeDtypeStruct((tok, width), bf16),) * 2,
        in_specs=[anywhere, anywhere, in_vmem, anywhere, anywhere, in_vmem],
        out_specs=(anywhere, anywhere),
        scratch_shapes=[
            pltpu.VMEM((2, GROUP, tok, width), bf16),
            pltpu.VMEM((2, GROUP, NY * cap, width), bf16),
            pltpu.VMEM((2, 2, NY * cap, width), bf16),
            pltpu.VMEM((2, tok, width), bf16),
            pltpu.VMEM((2, 2, NY * rows, width), bf16),
            pltpu.VMEM((2, 2, (NY - 1) * rows, width), bf16),
            pltpu.VMEM((2, 2, NY * rows, width), bf16),
            pltpu.VMEM((GROUP, 8, tok), jnp.float32),
            pltpu.VMEM((2, tok, width), bf16),
            pltpu.VMEM((2, tok, width), bf16),
            pltpu.VMEM((width, hidden), bf16),
            pltpu.VMEM((hidden, width), bf16),
            pltpu.VMEM((2, NY * rows, hidden), bf16),
            pltpu.VMEM((2, NY * rows, hidden), jnp.float32),
            pltpu.VMEM((2, GROUP, tok, NY * rows), bf16),
            pltpu.VMEM((NY * rows, NY * rows), bf16),
            pltpu.VMEM((GROUP, NY * cap, NY * rows), bf16),
            pltpu.VMEM((2, 2, NY * cap, tok), bf16),
            pltpu.VMEM((2, 2, tok, NY * cap), bf16),
            dma((2, 2, 4, 4)), dma((2, 2, 4, 4)),
            dma((3,)), dma((3,)),
            dma((2, 2, 2, 3)), dma((2, 2, 2, 3)),
            dma((2, 2, 2, 3)), dma((2, 2, 2, 3)),
            dma((2, 2, 4, 4)), dma((2, 2, 4, 4)),
            dma((2, 4)), dma((2, 4)),
            dma((4,)),
            pltpu.SemaphoreType.REGULAR((2,)),
        ],
        compiler_params=pltpu.CompilerParams(
            collective_id=0, has_side_effects=True, vmem_limit_bytes=62 * 1024 * 1024
        ),
        cost_estimate=pl.CostEstimate(
            flops=2 * 2 * 2 * NZ * NY * cap * width * hidden,
            bytes_accessed=16 * 1024 * 1024,
            transcendentals=0,
        ),
    )(xf, xr, norm_gain, upper, lower, info)
    return outf[None], outr[None]


def solution(mesh):
    return jax.shard_map(
        shards,
        mesh=mesh,
        in_specs=(
            P("pipe", "expert", None),
            P("pipe", "expert", None),
            P("pipe", None),
            P("pipe", "expert", None, None),
            P("pipe", "expert", None, None),
            P("pipe", None, "expert", None),
            P("pipe", None, "expert", None),
        ),
        out_specs=(P("pipe", "expert", None), P("pipe", "expert", None)),
        check_vma=False,
    )
```

time: 311 us -> 287 us (0.923)
  Pallas kernels: 304 us -> 280 us
    pallas_call x1, Pallas kernels: 304 us -> 280 us  [shards(): pl.pallas_call(functools.partial(kernel, cap), out_shape=(jax.ShapeDtypeS...]
where the time goes in v3:
time: 287 us
  Pallas kernels  280 us (98%)
  local copies, waits for them, and re-layouts  4.32 us (2%)
    pallas_call x1, Pallas kernels, shards(): pl.pallas_call(functools.partial(kernel, cap), out_shape=(jax.ShapeDtypeS...  280 us

profile of v3, /device:TPU:1, one launch (start us, length us, event | category | flops | bytes accessed | tf_op | source)
XLA Modules:
  0.0 286.8 jit_solution(5596404781064814592)
XLA Ops:
  0.6 0.7 convert_bitcast_fusion
  1.3 0.7 bitcast_convert_fusion
  2.0 0.6 pad_maximum_fusion
  2.6 279.9 %shard_map.86 = (bf16[128,3584]{1,0:T(8,128)(2,1)}, bf16[128,3584]{1,0:T(8,128)(2,1)}) custom-call(bf16[128,3584]{1,0:T(8,128)(2,1)} %bitcast.19, bf16[128,3584]{1,0:T(8,128)(2,1)} %bitcast.20, bf16[1,3584]{1,0:T(2,128)(2,1)} %gain_ref.1, bf16[3584,512]{1,0:T(8,128)(2,1)} %bitcast.17, bf16[512,3584]{1,0:T(8,128)(2,1)} %bitcast.18, f32[8,128]{1,0:T(8,128)} %bitcast.16), custom_call_target="tpu_custom_call" | custom-call | flops 9395240960 | bytes 16777216 | tf_op jit(solution)/shard_map/pallas_call | solution.py:517
  282.5 2.2 copy.11
  284.7 2.2 copy.12

commit v4 on v3

--- a/solution.py
+++ b/solution.py
@@ -30,8 +30,8 @@
     cap,
     xf_hbm, xr_hbm, gain_ref, up_hbm, down_hbm, info_ref,
     outf_ref, outr_ref,
-    ag, pkd, stag, tmp, inc, sel, ret, infos, xs, stage, up, down, act, hid,
-    gmat, order, leaf, pack, spread,
+    ag, pkd, stag, swap, tmp, inc, sel, ret, infos, xs, stage, up, down, act, parted, hid,
+    gmat, order, part, widen, leaf, pack, spread,
     ag_send, ag_recv, inf_send, inf_recv, yd_send, yd_recv, yr_send, yr_recv,
     rs_send, rs_recv, sh_send, sh_recv, load_sem, credit,
 ):
@@ -40,6 +40,8 @@
     quarter = width // 4
     rows = GROUP * cap
     slots = NY * cap
+    kept = parted.shape[0] - 2 * slots
+    pad = kept // NY
     per_y = NZ // SPLIT
     experts = NY * per_y
     p = lax.axis_index("pipe")
@@ -107,7 +109,9 @@
             }[hop]
         else:
             buf, src, dst = {
-                1: (ag, ag.at[s, 0], 1), 2: (pkd, stag.at[s, 0], 0), 3: (pkd, stag.at[s, 1], 1),
+                1: (ag, ag.at[s, 0], 1),
+                2: (pkd, stag.at[s, 0:slots], 0),
+                3: (pkd, stag.at[s, slots : 2 * slots], 1),
             }[hop]
         return remote(
             src.at[:, chunk(c)], buf.at[s, dst, :, chunk(c)],
@@ -130,7 +134,7 @@
 
     def pack_send(s, far, c):
         block = jnp.dot(pack[s, far], ag[s, 2 + far, :, chunk(c)], preferred_element_type=jnp.float32)
-        stag[s, far, :, chunk(c)] = block.astype(jnp.bfloat16)
+        stag[s, far * slots : (far + 1) * slots, chunk(c)] = block.astype(jnp.bfloat16)
         ag_copy(s, OUT, 2 + far, c).start()
 
     def second_hop(s, h):
@@ -181,10 +185,25 @@
         d, i, c = split_rows((NY * rows, NY * rows))
         column = lax.broadcasted_iota(jnp.int32, (NY * rows, NY * rows), 1)
         order[...] = jnp.where(column == i * slots + d * cap + c, 1.0, 0.0).astype(jnp.bfloat16)
-        _, d, c = split_rows((slots, NY * rows))
-        column = lax.broadcasted_iota(jnp.int32, (slots, NY * rows), 1)
-        for i in range(GROUP):
-            leaf[i] = jnp.where(column == d * rows + i * cap + c, 1.0, 0.0).astype(jnp.bfloat16)
+        r = lax.broadcasted_iota(jnp.int32, (kept, NY * rows), 0)
+        column = lax.broadcasted_iota(jnp.int32, (kept, NY * rows), 1)
+        d = sum(jnp.where(r >= k * pad, jnp.int32(1), jnp.int32(0)) for k in (1, 2, 3))
+        q = r - d * pad
+        part[0:kept] = jnp.where((column == d * rows + q) & (q < 2 * cap), 1.0, 0.0).astype(jnp.bfloat16)
+        r = lax.broadcasted_iota(jnp.int32, (2 * slots, NY * rows), 0)
+        column = lax.broadcasted_iota(jnp.int32, (2 * slots, NY * rows), 1)
+        d = sum(jnp.where(r >= k * 2 * cap, jnp.int32(1), jnp.int32(0)) for k in (1, 2, 3))
+        q = r - d * 2 * cap
+        part[kept:] = jnp.where(column == d * rows + 2 * cap + q, 1.0, 0.0).astype(jnp.bfloat16)
+        r = lax.broadcasted_iota(jnp.int32, (kept, 2 * slots), 0)
+        column = lax.broadcasted_iota(jnp.int32, (kept, 2 * slots), 1)
+        d = sum(jnp.where(r >= k * pad, jnp.int32(1), jnp.int32(0)) for k in (1, 2, 3))
+        q = r - d * pad
+        widen[...] = jnp.where((column == d * 2 * cap + q) & (q < 2 * cap), 1.0, 0.0).astype(jnp.bfloat16)
+        _, d, c = split_rows((slots, kept))
+        column = lax.broadcasted_iota(jnp.int32, (slots, kept), 1)
+        for i in (0, 1):
+            leaf[i] = jnp.where(column == d * pad + i * cap + c, 1.0, 0.0).astype(jnp.bfloat16)
 
     def hits_of(s, info, codes):
         hit0 = codes == info[4 * s : 4 * s + 1, :]
@@ -240,7 +259,8 @@
 
     def yr_copy(s, h, g, d):
         cols = pl.ds(h * half, half)
-        block = pl.ds(d * rows, rows)
+        many = rows if g == NEAR else pad
+        block = pl.ds(d * many, many)
         return remote(
             inc.at[s, g, block, cols], ret.at[s, g, block, cols],
             yr_send.at[s, h, g, d - 1], yr_recv.at[s, h, g, d - 1], ydev[NY - d],
@@ -264,35 +284,63 @@
 
         lax.fori_loop(0, half // tile, body, 0)
         if h == 1:
-            act[g] = jax.nn.silu(hid[g]).astype(jnp.bfloat16)
+            value = jax.nn.silu(hid[g]).astype(jnp.bfloat16)
+            if g == NEAR:
+                act[...] = value
+            else:
+                parted[...] = jnp.dot(part[...], value, preferred_element_type=jnp.float32).astype(
+                    jnp.bfloat16
+                )
 
     def lower(s, h, g):
         tile = tile_of(half)
 
         def body(j, carry):
             cols = pl.ds(pl.multiple_of(h * half + j * tile, 128), tile)
-            out = jnp.dot(act[g], down[:, cols], preferred_element_type=jnp.float32)
+            source = act if g == NEAR else parted
+            out = jnp.dot(source[...], down[:, cols], preferred_element_type=jnp.float32)
             out = out.astype(jnp.bfloat16)
-            ret[s, g, 0:rows, cols] = out[0:rows]
-            inc[s, g, rows:, cols] = out[rows:]
+            if g == NEAR:
+                ret[s, g, 0:rows, cols] = out[0:rows]
+                inc[s, g, rows:, cols] = out[rows:]
+            else:
+                inc[s, g, 0:kept, cols] = out[0:kept]
+                stag[s, :, cols] = out[kept:]
             return carry
 
         lax.fori_loop(0, half // tile, body, 0)
+        if g == NEAR:
+            for d in (2, 1, 3):
+                yr_copy(s, h, g, d).start()
+        else:
+            for c in chunks(h):
+                rs_copy(s, IN, 0, c).start()
+
+    def join(s, h):
+        for c in chunks(h):
+            rs_copy(s, IN, 0, c).wait_recv()
+            total = inc[s, FAR, 0:kept, chunk(c)].astype(jnp.float32) + jnp.dot(
+                widen[...], swap[s, :, chunk(c)], preferred_element_type=jnp.float32
+            )
+            total = total.astype(jnp.bfloat16)
+            ret[s, FAR, 0:pad, chunk(c)] = total[0:pad]
+            inc[s, FAR, pad:kept, chunk(c)] = total[pad:]
         for d in (2, 1, 3):
-            yr_copy(s, h, g, d).start()
+            yr_copy(s, h, FAR, d).start()
 
     def rs_copy(s, way, step, c):
         if way == IN:
-            buf, src, dst = {
-                0: (pkd, stag.at[s, 0], 1), 1: (pkd, stag.at[s, 1], 0),
-                2: (ag, ag.at[s, 3], 1), 3: (ag, tmp.at[s], 0),
+            src, dst = {
+                0: (stag.at[s], swap.at[s]),
+                2: (ag.at[s, 3], ag.at[s, 1]), 3: (tmp.at[s], ag.at[s, 0]),
             }[step]
         else:
-            buf, src, dst = {
-                0: (pkd, pkd.at[s, 1], 2), 1: (pkd, pkd.at[s, 0], 3), 2: (ag, ag.at[s, 1], 2),
+            src, dst = {
+                0: (pkd.at[s, 1], pkd.at[s, 2]), 1: (pkd.at[s, 0], pkd.at[s, 3]),
+                2: (ag.at[s, 1], ag.at[s, 2]),
             }[step]
         return remote(
-            src.at[:, chunk(c)], buf.at[s, dst, :, chunk(c)],
+            src.at[:, chunk(c)], dst.at[:, chunk(c)],
             rs_send.at[s, way, step, c], rs_recv.at[s, way, step, c], zdev[way],
         )
 
@@ -300,20 +348,13 @@
         return jnp.dot(gmat[s, i], ret[s, NEAR, :, chunk(c)], preferred_element_type=jnp.float32)
 
     def far_rows(s, i, c):
-        return jnp.dot(leaf[i], ret[s, FAR, :, chunk(c)], preferred_element_type=jnp.float32)
+        return jnp.dot(leaf[i], ret[s, FAR, 0:kept, chunk(c)], preferred_element_type=jnp.float32)
 
     def rs_begin(s, h):
-        for step, i in ((0, 3), (1, 2)):
+        for step in (0, 1):
             for c in chunks(h):
-                stag[s, step, :, chunk(c)] = far_rows(s, i, c).astype(jnp.bfloat16)
-                rs_copy(s, IN, step, c).start()
-
-    def pair_sum(s, step, c):
-        own = far_rows(s, 1 - step, c)
-        rs_copy(s, IN, step, c).wait_recv()
-        total = own + pkd[s, 1 - step, :, chunk(c)].astype(jnp.float32)
-        pkd[s, 1 - step, :, chunk(c)] = total.astype(jnp.bfloat16)
-        rs_copy(s, OUT, step, c).start()
+                pkd[s, 1 - step, :, chunk(c)] = far_rows(s, 1 - step, c).astype(jnp.bfloat16)
+                rs_copy(s, OUT, step, c).start()
 
     def spread_sum(s, step, c):
         own = near_rows(s, 3 - step, c)
@@ -334,20 +375,15 @@
         ag[s, 1, :, chunk(c)] = total.astype(jnp.bfloat16)
         rs_copy(s, OUT, 2, c).start()
 
-    def rs_mid_a(s, h):
-        for c in chunks(h):
-            pair_sum(s, 0, c)
-
-    def rs_mid_b(s, h):
+    def rs_two(s, h):
         for c in chunks(h):
             spread_sum(s, 0, c)
-            pair_sum(s, 1, c)
-
-    def rs_late_a(s, h):
+
+    def rs_one(s, h):
         for c in chunks(h):
             spread_sum(s, 1, c)
 
-    def rs_late_b(s, h):
+    def rs_pass(s, h):
         for c in chunks(h):
             pass_sum(s, c)
 
@@ -374,7 +410,7 @@
                     yd_copy(s, h, g, d).wait_send()
                     yr_copy(s, h, g, d).wait_send()
         for c in range(4):
-            for step in (0, 1, 2, 3):
+            for step in (0, 2, 3):
                 rs_copy(s, IN, step, c).wait_send()
             for step in (0, 1, 2):
                 rs_copy(s, OUT, step, c).wait_send()
@@ -399,7 +435,6 @@
     inf_copy(1).start()
     own_send(f, 0, (IN,))
     own_send(f, 0, (OUT,))
-    constants()
     load_up.start()
     load_down.start()
     inf_copy(1).wait_recv()
@@ -407,97 +442,115 @@
     inf_copy(0).wait_recv()
     pack_matrices(0)
     second_hop(f, 0)
+    own_send(f, 1, (OUT,))
+    load_xr.wait()
+    normalise(r)
     inf_copy(2).wait_recv()
     pack_matrices(1)
     third_hop(f, 0)
     select(f, 0, near)
+    own_send(f, 1, (IN,))
     fourth_hop(f, 0)
-    own_send(f, 1, (OUT,))
-    own_send(f, 1, (IN,))
-    load_xr.wait()
-    normalise(r)
+    second_hop(f, 1)
     gather_end(f, 0)
+    constants()
     select(f, 0, far)
-    second_hop(f, 1)
     third_hop(f, 1)
     select(f, 1, near)
+    own_send(r, 0, (OUT,))
     fourth_hop(f, 1)
+    own_send(r, 0, (IN,))
     load_up.wait()
     load_down.wait()
     upper(f, 0, near)
-    own_send(r, 0, (OUT,))
-    own_send(r, 1, (OUT,))
-    own_send(r, 0, (IN,))
+    upper(f, 0, far)
     gather_end(f, 1)
     select(f, 1, far)
     own_send(r, 1, (IN,))
-    upper(f, 0, far)
     upper(f, 1, near)
+    give_credit(f)
     lower(f, 1, near)
+    own_send(r, 1, (OUT,))
+    second_hop(r, 0)
+    second_hop(r, 1)
     upper(f, 1, far)
+    lower(f, 0, far)
     lower(f, 1, far)
-    second_hop(r, 1)
-    lower(f, 0, far)
-    second_hop(r, 0)
+    lower(f, 0, near)
+    third_hop(r, 1)
     third_hop(r, 0)
+    select(r, 0, near)
     fourth_hop(r, 0)
-    third_hop(r, 1)
-    select(r, 0, near)
-    fourth_hop(r, 1)
-    gather_end(r, 0)
-    give_credit(f)
-    lower(f, 0, near)
-    back(f, 1, far)
-    select(r, 0, far)
+    join(f, 0)
+    back(f, 1, near)
+    upper(r, 0, near)
+    join(f, 1)
+    back(f, 0, near)
     back(f, 0, far)
-    back(f, 1, near)
+    select(r, 1, near)
     pl.semaphore_wait(credit.at[f], 2)
     rs_begin(f, 0)
+    fourth_hop(r, 1)
+    back(f, 1, far)
+    rs_two(f, 0)
+    rs_begin(f, 1)
+    gather_end(r, 0)
+    select(r, 0, far)
     gather_end(r, 1)
-    rs_mid_a(f, 0)
-    upper(r, 0, near)
-    rs_begin(f, 1)
     select(r, 1, far)
-    back(f, 0, near)
-    rs_mid_a(f, 1)
-    rs_mid_b(f, 0)
-    rs_mid_b(f, 1)
-    select(r, 1, near)
+    rs_two(f, 1)
     upper(r, 0, far)
-    rs_late_a(f, 1)
+    give_credit(r)
+    rs_one(f, 1)
+    upper(r, 1, near)
     upper(r, 1, far)
     lower(r, 0, far)
-    rs_late_b(f, 1)
-    upper(r, 1, near)
-    give_credit(r)
-    rs_late_a(f, 0)
     lower(r, 0, near)
+    lower(r, 1, far)
+    rs_pass(f, 1)
+    rs_one(f, 0)
+    join(r, 0)
+    rs_pass(f, 0)
     rs_end(f, 1)
-    rs_late_b(f, 0)
     back(r, 0, far)
     pl.semaphore_wait(credit.at[r], 2)
     rs_begin(r, 0)
-    rs_mid_a(r, 0)
-    lower(r, 1, far)
+    join(r, 1)
     back(r, 0, near)
-    rs_mid_b(r, 0)
-    rs_late_a(r, 0)
-    rs_late_b(r, 0)
+    rs_two(r, 0)
     lower(r, 1, near)
+    rs_one(r, 0)
     back(r, 1, far)
     rs_begin(r, 1)
-    rs_mid_a(r, 1)
+    rs_pass(r, 0)
+    back(r, 1, near)
+    rs_two(r, 1)
     rs_end(f, 0)
-    back(r, 1, near)
-    rs_mid_b(r, 1)
-    rs_late_a(r, 1)
-    rs_late_b(r, 1)
+    rs_one(r, 1)
+    rs_pass(r, 1)
     rs_end(r, 0)
     rs_end(r, 1)
     for i in range(len(INFO)):
         inf_copy(i).wait_send()
     finish(f)
     finish(r)
+
+
+def settle(a_ref, b_ref, c_ref, d_ref, hold, into, out):
+    rows = a_ref.shape[0] // 4
+    steps = []
+    for n, (source, target) in enumerate(((a_ref, c_ref), (b_ref, d_ref))):
+        for i in range(4):
+            at = pl.ds(i * rows, rows)
+            first = pltpu.make_async_copy(source.at[at], hold.at[n, at], into.at[n, i])
+            second = pltpu.make_async_copy(hold.at[n, at], target.at[at], out.at[n, i])
+            first.start()
+            steps.append((first, second))
+    for first, second in steps:
+        first.wait()
+        second.start()
+    for _, second in steps:
+        second.wait()
 
 
 def shards(stream_fwd, stream_rev, norm_gain, w_up, w_down, routes, gates):
@@ -510,6 +563,7 @@
     info = jnp.concatenate([routes[0].astype(jnp.float32), gates[0].astype(jnp.float32)], axis=-1)
     info = info.transpose(0, 2, 1).reshape(8, tok)
     rows = GROUP * cap
+    kept = NY * (-(-2 * cap // 16) * 16)
     bf16 = jnp.bfloat16
     dma = pltpu.SemaphoreType.DMA
     anywhere = pl.BlockSpec(memory_space=pl.ANY)
@@ -522,7 +576,8 @@
         scratch_shapes=[
             pltpu.VMEM((2, GROUP, tok, width), bf16),
             pltpu.VMEM((2, GROUP, NY * cap, width), bf16),
-            pltpu.VMEM((2, 2, NY * cap, width), bf16),
+            pltpu.VMEM((2, 2 * NY * cap, width), bf16),
+            pltpu.VMEM((2, 2 * NY * cap, width), bf16),
             pltpu.VMEM((2, tok, width), bf16),
             pltpu.VMEM((2, 2, NY * rows, width), bf16),
             pltpu.VMEM((2, 2, (NY - 1) * rows, width), bf16),
@@ -532,11 +587,14 @@
             pltpu.VMEM((2, tok, width), bf16),
             pltpu.VMEM((width, hidden), bf16),
             pltpu.VMEM((hidden, width), bf16),
-            pltpu.VMEM((2, NY * rows, hidden), bf16),
+            pltpu.VMEM((NY * rows, hidden), bf16),
+            pltpu.VMEM((kept + 2 * NY * cap, hidden), bf16),
             pltpu.VMEM((2, NY * rows, hidden), jnp.float32),
             pltpu.VMEM((2, GROUP, tok, NY * rows), bf16),
             pltpu.VMEM((NY * rows, NY * rows), bf16),
-            pltpu.VMEM((GROUP, NY * cap, NY * rows), bf16),
+            pltpu.VMEM((kept + 2 * NY * cap, NY * rows), bf16),
+            pltpu.VMEM((kept, 2 * NY * cap), bf16),
+            pltpu.VMEM((2, NY * cap, kept), bf16),
             pltpu.VMEM((2, 2, NY * cap, tok), bf16),
             pltpu.VMEM((2, 2, tok, NY * cap), bf16),
             dma((2, 2, 4, 4)), dma((2, 2, 4, 4)),
@@ -557,6 +615,13 @@
             transcendentals=0,
         ),
     )(xf, xr, norm_gain, upper, lower, info)
+    outf, outr = pl.pallas_call(
+        settle,
+        out_shape=(jax.ShapeDtypeStruct((tok, width), bf16),) * 2,
+        in_specs=[anywhere, anywhere],
+        out_specs=(anywhere, anywhere),
+        scratch_shapes=[pltpu.VMEM((2, tok, width), bf16), dma((2, 4)), dma((2, 4))],
+    )(outf, outr)
     return outf[None], outr[None]
 
 

time: 287 us -> 278 us (0.969)
  Pallas kernels: 280 us -> 275 us
  local copies, waits for them, and re-layouts: 4.32 us -> 0 us
    pallas_call x1, Pallas kernels: 280 us -> 272 us  [shards(): pl.pallas_call(functools.partial(kernel, cap), out_shape=(jax.ShapeDtypeS...]
    unnamed x2 -> x0, local copies, waits for them, and re-layouts: 4.32 us -> none
where the time goes in v4:
time: 278 us
  Pallas kernels  275 us (99%)
    pallas_call x1, Pallas kernels, shards(): pl.pallas_call(functools.partial(kernel, cap), out_shape=(jax.ShapeDtypeS...  272 us

profile of v4, /device:TPU:1, one launch (start us, length us, event | category | flops | bytes accessed | tf_op | source)
XLA Modules:
  0.0 277.6 jit_solution(4967429366172137323)
XLA Ops:
  0.6 0.7 convert_bitcast_fusion
  1.3 0.7 bitcast_convert_fusion
  2.0 0.6 pad_maximum_fusion
  2.6 272.4 %shard_map.86 = (bf16[128,3584]{1,0:T(8,128)(2,1)}, bf16[128,3584]{1,0:T(8,128)(2,1)}) custom-call(bf16[128,3584]{1,0:T(8,128)(2,1)} %bitcast.17, bf16[128,3584]{1,0:T(8,128)(2,1)} %bitcast.18, bf16[1,3584]{1,0:T(2,128)(2,1)} %gain_ref.1, bf16[3584,512]{1,0:T(8,128)(2,1)} %bitcast.15, bf16[512,3584]{1,0:T(8,128)(2,1)} %bitcast.16, f32[8,128]{1,0:T(8,128)} %bitcast.14), custom_call_target="tpu_custom_call" | custom-call | flops 9395240960 | bytes 16777216 | tf_op jit(solution)/shard_map/pallas_call | solution.py:571
  275.1 2.4 shard_map.87

commit v5 on v4

--- a/solution.py
+++ b/solution.py
@@ -16,6 +16,7 @@
 
 IN, OUT = 0, 1
 NEAR, FAR = 0, 1
+WIDE = ((0, 1), (1, 0))
 
 
 def tile_of(width, most=512):
@@ -28,10 +29,10 @@
 
 def kernel(
     cap,
-    xf_hbm, xr_hbm, gain_ref, up_hbm, down_hbm, info_ref,
+    xf_hbm, xr_hbm, gain_ref, up_hbm, down_hbm, picks_ref, gates_ref,
     outf_ref, outr_ref,
-    ag, pkd, stag, swap, tmp, inc, sel, ret, infos, xs, stage, up, down, act, parted, hid,
-    gmat, order, part, widen, leaf, pack, spread,
+    ag, whole, pkd, stag, swap, tmp, inc, sel, ret, infos, xs, stage, up, down, act, parted, hid,
+    gmat, order, order2, part, widen, leaf, pack, spread,
     ag_send, ag_recv, inf_send, inf_recv, yd_send, yd_recv, yr_send, yr_recv,
     rs_send, rs_recv, sh_send, sh_recv, load_sem, credit,
 ):
@@ -93,32 +94,38 @@
         t1 = lax.broadcasted_iota(jnp.int32, (tok, tok), 1)
         earlier = jnp.where(t0 < t1, 1.0, 0.0).astype(jnp.bfloat16)
         for s in (0, 1):
-            hits = [here == info_ref[4 * s + k : 4 * s + k + 1, :] for k in range(TOPK)]
+            picks = picks_ref[s].astype(jnp.float32)
+            hits = [here == picks[k : k + 1, :] for k in range(TOPK)]
             named = jnp.where(hits[0] | hits[1], 1.0, 0.0).astype(jnp.bfloat16)
             before = jnp.dot(named, earlier, preferred_element_type=jnp.float32)
             for k in range(TOPK):
                 code = jnp.where(hits[k], here * cap + before, 0.0)
                 infos[0, 4 * s + k : 4 * s + k + 1, :] = jnp.sum(code, axis=0, keepdims=True)
-            infos[0, 4 * s + 2 : 4 * s + 4, :] = info_ref[4 * s + 2 : 4 * s + 4, :]
+            infos[0, 4 * s + 2 : 4 * s + 4, :] = gates_ref[s].astype(jnp.float32)
 
     def ag_copy(s, way, hop, c):
+        packed = (stag.at[s, 0:slots], stag.at[s, slots : 2 * slots])
         if way == IN:
-            buf, src, dst = {
-                1: (ag, ag.at[s, 0], 2), 2: (ag, ag.at[s, 1], 3),
-                3: (pkd, pkd.at[s, 0], 2), 4: (pkd, pkd.at[s, 1], 3),
-            }[hop]
+            plan = {
+                1: (ag.at[s, 0], ag.at[s, 2]), 2: (ag.at[s, 1], ag.at[s, 3]),
+                3: (pkd.at[s, 0], pkd.at[s, 2]), 4: (pkd.at[s, 1], pkd.at[s, 3]),
+            }
+            if (s, c // 2) in WIDE:
+                plan[3] = (whole.at[s, 0], whole.at[s, 1])
         else:
-            buf, src, dst = {
-                1: (ag, ag.at[s, 0], 1),
-                2: (pkd, stag.at[s, 0:slots], 0),
-                3: (pkd, stag.at[s, slots : 2 * slots], 1),
-            }[hop]
+            plan = {
+                1: (ag.at[s, 0], ag.at[s, 1]), 2: (packed[0], pkd.at[s, 0]), 3: (packed[1], pkd.at[s, 1]),
+            }
+            if (s, c // 2) in WIDE:
+                plan[2] = (ag.at[s, 2], whole.at[s, 0])
+                plan[4] = (packed[0], pkd.at[s, 3])
+        src, dst = plan[hop]
         return remote(
-            src.at[:, chunk(c)], buf.at[s, dst, :, chunk(c)],
+            src.at[:, chunk(c)], dst.at[:, chunk(c)],
             ag_send.at[s, way, hop - 1, c], ag_recv.at[s, way, hop - 1, c], zdev[way],
         )
 
-    INFO = ((IN, 0, 2), (OUT, 0, 1), (IN, 1, 3))
+    INFO = ((IN, 0, 2), (OUT, 0, 1), (IN, 1, 3), (OUT, 2, 4), (IN, 4, 5))
 
     def inf_copy(i):
         way, source, target = INFO[i]
@@ -133,8 +140,10 @@
                 ag_copy(s, way, 1, c).start()
 
     def pack_send(s, far, c):
-        block = jnp.dot(pack[s, far], ag[s, 2 + far, :, chunk(c)], preferred_element_type=jnp.float32)
-        stag[s, far * slots : (far + 1) * slots, chunk(c)] = block.astype(jnp.bfloat16)
+        block = whole[s, 1, :, chunk(c)] if far == 2 else ag[s, 2 + far, :, chunk(c)]
+        block = jnp.dot(pack[s, far], block, preferred_element_type=jnp.float32)
+        at = far % 2 * slots
+        stag[s, at : at + slots, chunk(c)] = block.astype(jnp.bfloat16)
         ag_copy(s, OUT, 2 + far, c).start()
 
     def second_hop(s, h):
@@ -142,7 +151,10 @@
             ag_copy(s, OUT, 1, c).wait_recv()
             ag_copy(s, IN, 2, c).start()
             ag_copy(s, IN, 1, c).wait_recv()
-            pack_send(s, 0, c)
+            if (s, h) in WIDE:
+                ag_copy(s, OUT, 2, c).start()
+            else:
+                pack_send(s, 0, c)
 
     def third_hop(s, h):
         for c in chunks(h):
@@ -153,20 +165,24 @@
 
     def fourth_hop(s, h):
         for c in chunks(h):
-            ag_copy(s, OUT, 3, c).wait_recv()
-            ag_copy(s, IN, 4, c).start()
+            if (s, h) in WIDE:
+                ag_copy(s, IN, 3, c).wait_recv()
+                pack_send(s, 2, c)
+            else:
+                ag_copy(s, OUT, 3, c).wait_recv()
+                ag_copy(s, IN, 4, c).start()
 
     def gather_end(s, h):
-        for hop in (3, 4):
-            for c in chunks(h):
-                ag_copy(s, IN, hop, c).wait_recv()
+        for c in chunks(h):
+            for hop in (3, 4):
+                ag_copy(s, OUT if (s, h) in WIDE else IN, hop, c).wait_recv()
 
     def gather_sent(s):
         for c in range(4):
-            for hop in (1, 2, 3, 4):
-                ag_copy(s, IN, hop, c).wait_send()
-            for hop in (1, 2, 3):
-                ag_copy(s, OUT, hop, c).wait_send()
+            last = OUT if (s, c // 2) in WIDE else IN
+            for way in (IN, OUT):
+                for hop in (1, 2, 3, 4) if way == last else (1, 2, 3):
+                    ag_copy(s, way, hop, c).wait_send()
 
     def split_rows(shape):
         r = lax.broadcasted_iota(jnp.int32, shape, 0)
@@ -185,6 +201,10 @@
         d, i, c = split_rows((NY * rows, NY * rows))
         column = lax.broadcasted_iota(jnp.int32, (NY * rows, NY * rows), 1)
         order[...] = jnp.where(column == i * slots + d * cap + c, 1.0, 0.0).astype(jnp.bfloat16)
+        d, i, c = split_rows((NY * rows, 2 * slots))
+        column = lax.broadcasted_iota(jnp.int32, (NY * rows, 2 * slots), 1)
+        at = jnp.where(i == 1, 0, slots) + d * cap + c
+        order2[...] = jnp.where((column == at) & ((i == 1) | (i == 3)), 1.0, 0.0).astype(jnp.bfloat16)
         r = lax.broadcasted_iota(jnp.int32, (kept, NY * rows), 0)
         column = lax.broadcasted_iota(jnp.int32, (kept, NY * rows), 1)
         d = sum(jnp.where(r >= k * pad, jnp.int32(1), jnp.int32(0)) for k in (1, 2, 3))
@@ -216,9 +236,11 @@
     def pack_matrices(far):
         _, d, c = split_rows((slots, tok))
         codes = (expert_at(d, z_out // SPLIT) * cap + c).astype(jnp.float32)
-        info = infos[2 + far]
+        info = infos[2 + far if far < 2 else 5]
         for s in (0, 1):
-            pack[s, far], spread[s, far] = hits_of(s, info, codes)
+            pack[s, far], weights = hits_of(s, info, codes)
+            if far < 2:
+                spread[s, far] = weights
 
     def select(s, h, g):
         if g == NEAR:
@@ -231,16 +253,29 @@
                 if h == 0:
                     gmat[s, i] = weights
             pick = jnp.concatenate(parts, axis=1)
-            source, depth = ag, tok
-        else:
-            pick = order[...]
-            source, depth = pkd, slots
+        elif (s, h) in WIDE:
+            d, at, c = split_rows((NY * rows, tok))
+            codes = (expert_at(d, z // SPLIT) * cap + c).astype(jnp.float32)
+            parts = [
+                hits_of(s, infos[4 + n], jnp.where(at == 2 * n, codes, -1.0))[0] for n in (0, 1)
+            ]
+            pick = jnp.concatenate(parts, axis=1)
         tile = tile_of(half)
 
         def body(j, carry):
             cols = pl.ds(pl.multiple_of(h * half + j * tile, 128), tile)
-            block = source[s, :, :, cols].reshape(GROUP * depth, tile)
-            out = jnp.dot(pick, block, preferred_element_type=jnp.float32).astype(jnp.bfloat16)
+            if g == NEAR:
+                block = ag[s, :, :, cols].reshape(GROUP * tok, tile)
+                out = jnp.dot(pick, block, preferred_element_type=jnp.float32)
+            elif (s, h) in WIDE:
+                block = whole[s, :, :, cols].reshape(2 * tok, tile)
+                out = jnp.dot(pick, block, preferred_element_type=jnp.float32)
+                block = jnp.concatenate([pkd[s, 1, :, cols], pkd[s, 3, :, cols]], axis=0)
+                out = out + jnp.dot(order2[...], block, preferred_element_type=jnp.float32)
+            else:
+                block = pkd[s, :, :, cols].reshape(GROUP * slots, tile)
+                out = jnp.dot(order[...], block, preferred_element_type=jnp.float32)
+            out = out.astype(jnp.bfloat16)
             inc[s, g, 0:rows, cols] = out[0:rows]
             sel[s, g, :, cols] = out[rows:]
             return carry
@@ -435,100 +470,105 @@
     inf_copy(1).start()
     own_send(f, 0, (IN,))
     own_send(f, 0, (OUT,))
+    own_send(f, 1, (IN,))
     load_up.start()
     load_down.start()
     inf_copy(1).wait_recv()
     inf_copy(2).start()
     inf_copy(0).wait_recv()
+    inf_copy(3).start()
     pack_matrices(0)
+    constants()
+    own_send(f, 1, (OUT,))
     second_hop(f, 0)
-    own_send(f, 1, (OUT,))
-    load_xr.wait()
-    normalise(r)
+    second_hop(f, 1)
     inf_copy(2).wait_recv()
+    inf_copy(3).wait_recv()
+    inf_copy(4).start()
     pack_matrices(1)
     third_hop(f, 0)
     select(f, 0, near)
-    own_send(f, 1, (IN,))
     fourth_hop(f, 0)
-    second_hop(f, 1)
-    gather_end(f, 0)
-    constants()
-    select(f, 0, far)
+    inf_copy(4).wait_recv()
+    pack_matrices(2)
     third_hop(f, 1)
     select(f, 1, near)
+    load_xr.wait()
+    normalise(r)
     own_send(r, 0, (OUT,))
+    gather_end(f, 0)
+    own_send(r, 1, (IN,))
+    select(f, 0, far)
     fourth_hop(f, 1)
-    own_send(r, 0, (IN,))
     load_up.wait()
     load_down.wait()
     upper(f, 0, near)
-    upper(f, 0, far)
     gather_end(f, 1)
+    upper(f, 1, near)
+    own_send(r, 0, (IN,))
     select(f, 1, far)
-    own_send(r, 1, (IN,))
-    upper(f, 1, near)
+    second_hop(r, 0)
+    own_send(r, 1, (OUT,))
+    lower(f, 0, near)
     give_credit(f)
     lower(f, 1, near)
-    own_send(r, 1, (OUT,))
-    second_hop(r, 0)
-    second_hop(r, 1)
+    third_hop(r, 0)
+    upper(f, 0, far)
     upper(f, 1, far)
     lower(f, 0, far)
-    lower(f, 1, far)
-    lower(f, 0, near)
-    third_hop(r, 1)
-    third_hop(r, 0)
+    second_hop(r, 1)
     select(r, 0, near)
     fourth_hop(r, 0)
     join(f, 0)
-    back(f, 1, near)
+    gather_end(r, 0)
+    lower(f, 1, far)
     upper(r, 0, near)
+    third_hop(r, 1)
+    back(f, 0, near)
+    select(r, 0, far)
+    back(f, 0, far)
+    fourth_hop(r, 1)
     join(f, 1)
-    back(f, 0, near)
-    back(f, 0, far)
-    select(r, 1, near)
     pl.semaphore_wait(credit.at[f], 2)
     rs_begin(f, 0)
-    fourth_hop(r, 1)
-    back(f, 1, far)
     rs_two(f, 0)
-    rs_begin(f, 1)
-    gather_end(r, 0)
-    select(r, 0, far)
     gather_end(r, 1)
     select(r, 1, far)
+    upper(r, 0, far)
+    back(f, 1, near)
+    back(f, 1, far)
+    rs_one(f, 0)
+    rs_begin(f, 1)
+    select(r, 1, near)
     rs_two(f, 1)
-    upper(r, 0, far)
     give_credit(r)
-    rs_one(f, 1)
-    upper(r, 1, near)
     upper(r, 1, far)
     lower(r, 0, far)
+    lower(r, 1, far)
+    upper(r, 1, near)
     lower(r, 0, near)
-    lower(r, 1, far)
+    rs_pass(f, 0)
+    rs_one(f, 1)
+    join(r, 0)
     rs_pass(f, 1)
-    rs_one(f, 0)
-    join(r, 0)
-    rs_pass(f, 0)
-    rs_end(f, 1)
+    rs_end(f, 0)
+    join(r, 1)
     back(r, 0, far)
+    back(r, 0, near)
     pl.semaphore_wait(credit.at[r], 2)
     rs_begin(r, 0)
-    join(r, 1)
-    back(r, 0, near)
+    lower(r, 1, near)
     rs_two(r, 0)
-    lower(r, 1, near)
-    rs_one(r, 0)
     back(r, 1, far)
     rs_begin(r, 1)
-    rs_pass(r, 0)
+    rs_one(r, 0)
     back(r, 1, near)
     rs_two(r, 1)
-    rs_end(f, 0)
+    rs_pass(r, 0)
     rs_one(r, 1)
     rs_pass(r, 1)
     rs_end(r, 0)
+    rs_end(f, 1)
     rs_end(r, 1)
     for i in range(len(INFO)):
         inf_copy(i).wait_send()
@@ -560,8 +600,7 @@
     hidden = upper.shape[1]
     experts = lax.axis_size("expert") // SPLIT
     cap = SPLIT * max(1, tok * TOPK * 5 // (4 * SPLIT * experts))
-    info = jnp.concatenate([routes[0].astype(jnp.float32), gates[0].astype(jnp.float32)], axis=-1)
-    info = info.transpose(0, 2, 1).reshape(8, tok)
+    picks, weights = routes[0].transpose(0, 2, 1), gates[0].transpose(0, 2, 1)
     rows = GROUP * cap
     kept = NY * (-(-2 * cap // 16) * 16)
     bf16 = jnp.bfloat16
@@ -571,10 +610,11 @@
     outf, outr = pl.pallas_call(
         functools.partial(kernel, cap),
         out_shape=(jax.ShapeDtypeStruct((tok, width), bf16),) * 2,
-        in_specs=[anywhere, anywhere, in_vmem, anywhere, anywhere, in_vmem],
+        in_specs=[anywhere, anywhere, in_vmem, anywhere, anywhere, in_vmem, in_vmem],
         out_specs=(anywhere, anywhere),
         scratch_shapes=[
             pltpu.VMEM((2, GROUP, tok, width), bf16),
+            pltpu.VMEM((2, 2, tok, width), bf16),
             pltpu.VMEM((2, GROUP, NY * cap, width), bf16),
             pltpu.VMEM((2, 2 * NY * cap, width), bf16),
             pltpu.VMEM((2, 2 * NY * cap, width), bf16),
@@ -582,7 +622,7 @@
             pltpu.VMEM((2, 2, NY * rows, width), bf16),
             pltpu.VMEM((2, 2, (NY - 1) * rows, width), bf16),
             pltpu.VMEM((2, 2, NY * rows, width), bf16),
-            pltpu.VMEM((GROUP, 8, tok), jnp.float32),
+            pltpu.VMEM((6, 8, tok), jnp.float32),
             pltpu.VMEM((2, tok, width), bf16),
             pltpu.VMEM((2, tok, width), bf16),
             pltpu.VMEM((width, hidden), bf16),
@@ -592,13 +632,14 @@
             pltpu.VMEM((2, NY * rows, hidden), jnp.float32),
             pltpu.VMEM((2, GROUP, tok, NY * rows), bf16),
             pltpu.VMEM((NY * rows, NY * rows), bf16),
+            pltpu.VMEM((NY * rows, 2 * NY * cap), bf16),
             pltpu.VMEM((kept + 2 * NY * cap, NY * rows), bf16),
             pltpu.VMEM((kept, 2 * NY * cap), bf16),
             pltpu.VMEM((2, NY * cap, kept), bf16),
-            pltpu.VMEM((2, 2, NY * cap, tok), bf16),
+            pltpu.VMEM((2, 3, NY * cap, tok), bf16),
             pltpu.VMEM((2, 2, tok, NY * cap), bf16),
             dma((2, 2, 4, 4)), dma((2, 2, 4, 4)),
-            dma((3,)), dma((3,)),
+            dma((5,)), dma((5,)),
             dma((2, 2, 2, 3)), dma((2, 2, 2, 3)),
             dma((2, 2, 2, 3)), dma((2, 2, 2, 3)),
             dma((2, 2, 4, 4)), dma((2, 2, 4, 4)),
@@ -614,7 +655,7 @@
             bytes_accessed=16 * 1024 * 1024,
             transcendentals=0,
         ),
-    )(xf, xr, norm_gain, upper, lower, info)
+    )(xf, xr, norm_gain, upper, lower, picks, weights)
     outf, outr = pl.pallas_call(
         settle,
         out_shape=(jax.ShapeDtypeStruct((tok, width), bf16),) * 2,

time: 278 us -> 272 us (0.978)
  Pallas kernels: 275 us -> 271 us
    pallas_call x1, Pallas kernels: 272 us -> 268 us  [shards(): pl.pallas_call(functools.partial(kernel, cap), out_shape=(jax.ShapeDtypeS...]
where the time goes in v5:
time: 272 us
  Pallas kernels  271 us (100%)
    pallas_call x1, Pallas kernels, shards(): pl.pallas_call(functools.partial(kernel, cap), out_shape=(jax.ShapeDtypeS...  268 us

profile of v5, /device:TPU:1, one launch (start us, length us, event | category | flops | bytes accessed | tf_op | source)
XLA Modules:
  0.0 271.6 jit_solution(6074124106453493509)
XLA Ops:
  0.6 268.4 %shard_map.86 = (bf16[128,3584]{1,0:T(8,128)(2,1)}, bf16[128,3584]{1,0:T(8,128)(2,1)}) custom-call(bf16[128,3584]{1,0:T(8,128)(2,1)} %bitcast.14, bf16[128,3584]{1,0:T(8,128)(2,1)} %bitcast.15, bf16[1,3584]{1,0:T(2,128)(2,1)} %gain_ref.1, bf16[3584,512]{1,0:T(8,128)(2,1)} %bitcast.12, bf16[512,3584]{1,0:T(8,128)(2,1)} %bitcast.13, s32[2,2,128]{2,1,0:T(2,128)} %bitcast.18, ...), custom_call_target="tpu_custom_call" | custom-call | flops 9395240960 | bytes 16777216 | tf_op jit(solution)/shard_map/pallas_call | solution.py:610
  269.0 2.4 shard_map.87

commit v6 on v5

--- a/solution.py
+++ b/solution.py
@@ -134,6 +134,16 @@
     def chunks(h):
         return (2 * h, 2 * h + 1)
 
+    cut = quarter // 256 * 128 + (quarter // 128) % 2 * 128
+
+    def pieces(h):
+        return (0, 1) if h == 0 else (2, 3, 4)
+
+    def piece(c):
+        if c < 3:
+            return chunk(c)
+        return pl.ds(3 * quarter, cut) if c == 3 else pl.ds(3 * quarter + cut, quarter - cut)
+
     def own_send(s, h, ways):
         for c in chunks(h):
             for way in ways:
@@ -348,18 +358,18 @@
             for d in (2, 1, 3):
                 yr_copy(s, h, g, d).start()
         else:
-            for c in chunks(h):
+            for c in pieces(h):
                 rs_copy(s, IN, 0, c).start()
 
     def join(s, h):
-        for c in chunks(h):
+        for c in pieces(h):
             rs_copy(s, IN, 0, c).wait_recv()
-            total = inc[s, FAR, 0:kept, chunk(c)].astype(jnp.float32) + jnp.dot(
-                widen[...], swap[s, :, chunk(c)], preferred_element_type=jnp.float32
+            total = inc[s, FAR, 0:kept, piece(c)].astype(jnp.float32) + jnp.dot(
+                widen[...], swap[s, :, piece(c)], preferred_element_type=jnp.float32
             )
             total = total.astype(jnp.bfloat16)
-            ret[s, FAR, 0:pad, chunk(c)] = total[0:pad]
-            inc[s, FAR, pad:kept, chunk(c)] = total[pad:]
+            ret[s, FAR, 0:pad, piece(c)] = total[0:pad]
+            inc[s, FAR, pad:kept, piece(c)] = total[pad:]
         for d in (2, 1, 3):
             yr_copy(s, h, FAR, d).start()
 
@@ -375,67 +385,67 @@
                 2: (ag.at[s, 1], ag.at[s, 2]),
             }[step]
         return remote(
-            src.at[:, chunk(c)], dst.at[:, chunk(c)],
+            src.at[:, piece(c)], dst.at[:, piece(c)],
             rs_send.at[s, way, step, c], rs_recv.at[s, way, step, c], zdev[way],
         )
 
     def near_rows(s, i, c):
-        return jnp.dot(gmat[s, i], ret[s, NEAR, :, chunk(c)], preferred_element_type=jnp.float32)
+        return jnp.dot(gmat[s, i], ret[s, NEAR, :, piece(c)], preferred_element_type=jnp.float32)
 
     def far_rows(s, i, c):
-        return jnp.dot(leaf[i], ret[s, FAR, 0:kept, chunk(c)], preferred_element_type=jnp.float32)
+        return jnp.dot(leaf[i], ret[s, FAR, 0:kept, piece(c)], preferred_element_type=jnp.float32)
 
     def rs_begin(s, h):
         for step in (0, 1):
-            for c in chunks(h):
-                pkd[s, 1 - step, :, chunk(c)] = far_rows(s, 1 - step, c).astype(jnp.bfloat16)
+            for c in pieces(h):
+                pkd[s, 1 - step, :, piece(c)] = far_rows(s, 1 - step, c).astype(jnp.bfloat16)
                 rs_copy(s, OUT, step, c).start()
 
     def spread_sum(s, step, c):
         own = near_rows(s, 3 - step, c)
         rs_copy(s, OUT, step, c).wait_recv()
         total = own + jnp.dot(
-            spread[s, 1 - step], pkd[s, 2 + step, :, chunk(c)], preferred_element_type=jnp.float32
+            spread[s, 1 - step], pkd[s, 2 + step, :, piece(c)], preferred_element_type=jnp.float32
         )
         if step == 0:
-            ag[s, 3, :, chunk(c)] = total.astype(jnp.bfloat16)
+            ag[s, 3, :, piece(c)] = total.astype(jnp.bfloat16)
         else:
-            tmp[s, :, chunk(c)] = total.astype(jnp.bfloat16)
+            tmp[s, :, piece(c)] = total.astype(jnp.bfloat16)
         rs_copy(s, IN, 2 + step, c).start()
 
     def pass_sum(s, c):
         own = near_rows(s, 1, c)
         rs_copy(s, IN, 2, c).wait_recv()
-        total = own + ag[s, 1, :, chunk(c)].astype(jnp.float32)
-        ag[s, 1, :, chunk(c)] = total.astype(jnp.bfloat16)
+        total = own + ag[s, 1, :, piece(c)].astype(jnp.float32)
+        ag[s, 1, :, piece(c)] = total.astype(jnp.bfloat16)
         rs_copy(s, OUT, 2, c).start()
 
     def rs_two(s, h):
-        for c in chunks(h):
+        for c in pieces(h):
             spread_sum(s, 0, c)
 
     def rs_one(s, h):
-        for c in chunks(h):
+        for c in pieces(h):
             spread_sum(s, 1, c)
 
     def rs_pass(s, h):
-        for c in chunks(h):
+        for c in pieces(h):
             pass_sum(s, c)
 
     def sh_copy(s, c):
         return remote(
-            stage.at[s, :, chunk(c)], outs[s].at[:, chunk(c)], sh_send.at[s, c], sh_recv.at[s, c], pdev[s]
+            stage.at[s, :, piece(c)], outs[s].at[:, piece(c)], sh_send.at[s, c], sh_recv.at[s, c], pdev[s]
         )
 
     def rs_end(s, h):
-        for c in chunks(h):
-            own = near_rows(s, 0, c) + xs[s, :, chunk(c)].astype(jnp.float32)
+        for c in pieces(h):
+            own = near_rows(s, 0, c) + xs[s, :, piece(c)].astype(jnp.float32)
             rs_copy(s, OUT, 2, c).wait_recv()
             rs_copy(s, IN, 3, c).wait_recv()
             total = own + (
-                ag[s, 0, :, chunk(c)].astype(jnp.float32) + ag[s, 2, :, chunk(c)].astype(jnp.float32)
+                ag[s, 0, :, piece(c)].astype(jnp.float32) + ag[s, 2, :, piece(c)].astype(jnp.float32)
             )
-            stage[s, :, chunk(c)] = total.astype(jnp.bfloat16)
+            stage[s, :, piece(c)] = total.astype(jnp.bfloat16)
             sh_copy(s, c).start()
 
     def finish(s):
@@ -444,7 +454,7 @@
                 for d in (1, 2, 3):
                     yd_copy(s, h, g, d).wait_send()
                     yr_copy(s, h, g, d).wait_send()
-        for c in range(4):
+        for c in range(5):
             for step in (0, 2, 3):
                 rs_copy(s, IN, step, c).wait_send()
             for step in (0, 1, 2):
@@ -470,7 +480,8 @@
     inf_copy(1).start()
     own_send(f, 0, (IN,))
     own_send(f, 0, (OUT,))
-    own_send(f, 1, (IN,))
+    own_send(f, 1, (OUT,))
+    constants()
     load_up.start()
     load_down.start()
     inf_copy(1).wait_recv()
@@ -478,23 +489,23 @@
     inf_copy(0).wait_recv()
     inf_copy(3).start()
     pack_matrices(0)
-    constants()
-    own_send(f, 1, (OUT,))
+    own_send(f, 1, (IN,))
     second_hop(f, 0)
-    second_hop(f, 1)
     inf_copy(2).wait_recv()
     inf_copy(3).wait_recv()
     inf_copy(4).start()
     pack_matrices(1)
+    second_hop(f, 1)
     third_hop(f, 0)
     select(f, 0, near)
     fourth_hop(f, 0)
     inf_copy(4).wait_recv()
     pack_matrices(2)
     third_hop(f, 1)
-    select(f, 1, near)
     load_xr.wait()
     normalise(r)
+    own_send(r, 0, (IN,))
+    select(f, 1, near)
     own_send(r, 0, (OUT,))
     gather_end(f, 0)
     own_send(r, 1, (IN,))
@@ -503,68 +514,67 @@
     load_up.wait()
     load_down.wait()
     upper(f, 0, near)
+    upper(f, 1, near)
+    lower(f, 1, near)
     gather_end(f, 1)
-    upper(f, 1, near)
-    own_send(r, 0, (IN,))
-    select(f, 1, far)
     second_hop(r, 0)
     own_send(r, 1, (OUT,))
+    select(f, 1, far)
+    third_hop(r, 0)
     lower(f, 0, near)
+    back(f, 1, near)
+    second_hop(r, 1)
     give_credit(f)
-    lower(f, 1, near)
-    third_hop(r, 0)
+    select(r, 0, near)
     upper(f, 0, far)
+    fourth_hop(r, 0)
     upper(f, 1, far)
     lower(f, 0, far)
-    second_hop(r, 1)
-    select(r, 0, near)
-    fourth_hop(r, 0)
+    third_hop(r, 1)
+    gather_end(r, 0)
+    fourth_hop(r, 1)
+    lower(f, 1, far)
     join(f, 0)
-    gather_end(r, 0)
-    lower(f, 1, far)
-    upper(r, 0, near)
-    third_hop(r, 1)
-    back(f, 0, near)
     select(r, 0, far)
     back(f, 0, far)
-    fourth_hop(r, 1)
-    join(f, 1)
     pl.semaphore_wait(credit.at[f], 2)
     rs_begin(f, 0)
-    rs_two(f, 0)
     gather_end(r, 1)
     select(r, 1, far)
+    back(f, 0, near)
+    rs_two(f, 0)
+    rs_one(f, 0)
+    join(f, 1)
+    select(r, 1, near)
     upper(r, 0, far)
-    back(f, 1, near)
-    back(f, 1, far)
-    rs_one(f, 0)
-    rs_begin(f, 1)
-    select(r, 1, near)
-    rs_two(f, 1)
+    upper(r, 0, near)
+    rs_pass(f, 0)
     give_credit(r)
     upper(r, 1, far)
     lower(r, 0, far)
     lower(r, 1, far)
+    back(f, 1, far)
+    rs_begin(f, 1)
+    rs_end(f, 0)
+    join(r, 0)
     upper(r, 1, near)
     lower(r, 0, near)
-    rs_pass(f, 0)
-    rs_one(f, 1)
-    join(r, 0)
-    rs_pass(f, 1)
-    rs_end(f, 0)
-    join(r, 1)
+    rs_two(f, 1)
     back(r, 0, far)
-    back(r, 0, near)
     pl.semaphore_wait(credit.at[r], 2)
     rs_begin(r, 0)
+    rs_one(f, 1)
+    join(r, 1)
+    rs_pass(f, 1)
+    back(r, 0, near)
     lower(r, 1, near)
     rs_two(r, 0)
+    rs_one(r, 0)
     back(r, 1, far)
     rs_begin(r, 1)
-    rs_one(r, 0)
+    rs_pass(r, 0)
     back(r, 1, near)
     rs_two(r, 1)
-    rs_pass(r, 0)
     rs_one(r, 1)
     rs_pass(r, 1)
     rs_end(r, 0)
@@ -574,23 +584,6 @@
         inf_copy(i).wait_send()
     finish(f)
     finish(r)
-
-
-def settle(a_ref, b_ref, c_ref, d_ref, hold, into, out):
-    rows = a_ref.shape[0] // 4
-    steps = []
-    for n, (source, target) in enumerate(((a_ref, c_ref), (b_ref, d_ref))):
-        for i in range(4):
-            at = pl.ds(i * rows, rows)
-            first = pltpu.make_async_copy(source.at[at], hold.at[n, at], into.at[n, i])
-            second = pltpu.make_async_copy(hold.at[n, at], target.at[at], out.at[n, i])
-            first.start()
-            steps.append((first, second))
-    for first, second in steps:
-        first.wait()
-        second.start()
-    for _, second in steps:
-        second.wait()
 
 
 def shards(stream_fwd, stream_rev, norm_gain, w_up, w_down, routes, gates):
@@ -609,9 +602,9 @@
     in_vmem = pl.BlockSpec(memory_space=pltpu.VMEM)
     outf, outr = pl.pallas_call(
         functools.partial(kernel, cap),
-        out_shape=(jax.ShapeDtypeStruct((tok, width), bf16),) * 2,
+        out_shape=(pltpu.VMEM((tok, width), bf16),) * 2,
         in_specs=[anywhere, anywhere, in_vmem, anywhere, anywhere, in_vmem, in_vmem],
-        out_specs=(anywhere, anywhere),
+        out_specs=(in_vmem, in_vmem),
         scratch_shapes=[
             pltpu.VMEM((2, GROUP, tok, width), bf16),
             pltpu.VMEM((2, 2, tok, width), bf16),
@@ -642,8 +635,8 @@
             dma((5,)), dma((5,)),
             dma((2, 2, 2, 3)), dma((2, 2, 2, 3)),
             dma((2, 2, 2, 3)), dma((2, 2, 2, 3)),
-            dma((2, 2, 4, 4)), dma((2, 2, 4, 4)),
-            dma((2, 4)), dma((2, 4)),
+            dma((2, 2, 4, 5)), dma((2, 2, 4, 5)),
+            dma((2, 5)), dma((2, 5)),
             dma((4,)),
             pltpu.SemaphoreType.REGULAR((2,)),
         ],
@@ -656,13 +649,6 @@
             transcendentals=0,
         ),
     )(xf, xr, norm_gain, upper, lower, picks, weights)
-    outf, outr = pl.pallas_call(
-        settle,
-        out_shape=(jax.ShapeDtypeStruct((tok, width), bf16),) * 2,
-        in_specs=[anywhere, anywhere],
-        out_specs=(anywhere, anywhere),
-        scratch_shapes=[pltpu.VMEM((2, tok, width), bf16), dma((2, 4)), dma((2, 4))],
-    )(outf, outr)
     return outf[None], outr[None]
 
 

time: 272 us -> 271 us (level)
  Pallas kernels: 271 us -> 268 us
    pallas_call x2 -> x1, Pallas kernels: 271 us -> 268 us  [shards(): pl.pallas_call(functools.partial(kernel, cap), out_shape=(pltpu.VMEM((tok...]
where the time goes in v6:
time: 271 us; the launch traced here: 270 us
  Pallas kernels  268 us (99%)
    pallas_call x1, Pallas kernels, shards(): pl.pallas_call(functools.partial(kernel, cap), out_shape=(pltpu.VMEM((tok...  268 us

profile of v6, /device:TPU:1, one launch (start us, length us, event | category | flops | bytes accessed | tf_op | source)
XLA Modules:
  0.0 270.5 jit_solution(15790497280075363411)
XLA Ops:
  0.6 268.0 %shard_map.86 = (bf16[128,3584]{1,0:T(8,128)(2,1)S(1)}, bf16[128,3584]{1,0:T(8,128)(2,1)S(1)}) custom-call(bf16[128,3584]{1,0:T(8,128)(2,1)} %bitcast.16, bf16[128,3584]{1,0:T(8,128)(2,1)} %bitcast.17, bf16[1,3584]{1,0:T(2,128)(2,1)} %gain_ref.1, bf16[3584,512]{1,0:T(8,128)(2,1)} %bitcast.14, bf16[512,3584]{1,0:T(8,128)(2,1)} %bitcast.15, ...), custom_call_target="tpu_custom_call" | custom-call | flops 9395240960 | bytes 16777216 | tf_op jit(solution)/shard_map/pallas_call | solution.py:603
  268.6 0.9 copy.11
  269.5 0.9 copy.12

commit v7 on v6

--- a/solution.py
+++ b/solution.py
@@ -16,7 +16,7 @@
 
 IN, OUT = 0, 1
 NEAR, FAR = 0, 1
-WIDE = ((0, 1), (1, 0))
+WIDE = ((0, 1), (1, 0), (1, 1))
 
 
 def tile_of(width, most=512):
@@ -480,8 +480,6 @@
     inf_copy(1).start()
     own_send(f, 0, (IN,))
     own_send(f, 0, (OUT,))
-    own_send(f, 1, (OUT,))
-    constants()
     load_up.start()
     load_down.start()
     inf_copy(1).wait_recv()
@@ -489,96 +487,98 @@
     inf_copy(0).wait_recv()
     inf_copy(3).start()
     pack_matrices(0)
+    second_hop(f, 0)
     own_send(f, 1, (IN,))
-    second_hop(f, 0)
+    own_send(f, 1, (OUT,))
+    constants()
     inf_copy(2).wait_recv()
     inf_copy(3).wait_recv()
     inf_copy(4).start()
     pack_matrices(1)
+    third_hop(f, 0)
+    load_xr.wait()
+    normalise(r)
     second_hop(f, 1)
-    third_hop(f, 0)
+    fourth_hop(f, 0)
     select(f, 0, near)
-    fourth_hop(f, 0)
     inf_copy(4).wait_recv()
     pack_matrices(2)
     third_hop(f, 1)
-    load_xr.wait()
-    normalise(r)
+    own_send(r, 0, (OUT,))
+    select(f, 1, near)
     own_send(r, 0, (IN,))
-    select(f, 1, near)
-    own_send(r, 0, (OUT,))
-    gather_end(f, 0)
-    own_send(r, 1, (IN,))
-    select(f, 0, far)
-    fourth_hop(f, 1)
     load_up.wait()
     load_down.wait()
     upper(f, 0, near)
+    gather_end(f, 0)
+    select(f, 0, far)
+    fourth_hop(f, 1)
+    own_send(r, 1, (OUT,))
     upper(f, 1, near)
+    second_hop(r, 0)
+    gather_end(f, 1)
+    lower(f, 0, near)
+    select(f, 1, far)
     lower(f, 1, near)
-    gather_end(f, 1)
-    second_hop(r, 0)
-    own_send(r, 1, (OUT,))
-    select(f, 1, far)
+    own_send(r, 1, (IN,))
     third_hop(r, 0)
-    lower(f, 0, near)
-    back(f, 1, near)
     second_hop(r, 1)
     give_credit(f)
+    fourth_hop(r, 0)
+    upper(f, 0, far)
+    upper(f, 1, far)
     select(r, 0, near)
-    upper(f, 0, far)
-    fourth_hop(r, 0)
-    upper(f, 1, far)
     lower(f, 0, far)
+    back(f, 1, near)
     third_hop(r, 1)
+    lower(f, 1, far)
     gather_end(r, 0)
-    fourth_hop(r, 1)
-    lower(f, 1, far)
     join(f, 0)
     select(r, 0, far)
+    back(f, 0, near)
+    fourth_hop(r, 1)
     back(f, 0, far)
     pl.semaphore_wait(credit.at[f], 2)
     rs_begin(f, 0)
     gather_end(r, 1)
     select(r, 1, far)
-    back(f, 0, near)
     rs_two(f, 0)
+    join(f, 1)
+    upper(r, 0, far)
+    select(r, 1, near)
+    give_credit(r)
     rs_one(f, 0)
-    join(f, 1)
-    select(r, 1, near)
-    upper(r, 0, far)
-    upper(r, 0, near)
-    rs_pass(f, 0)
-    give_credit(r)
     upper(r, 1, far)
     lower(r, 0, far)
-    lower(r, 1, far)
+    upper(r, 0, near)
     back(f, 1, far)
     rs_begin(f, 1)
-    rs_end(f, 0)
+    rs_pass(f, 0)
+    lower(r, 1, far)
     join(r, 0)
     upper(r, 1, near)
     lower(r, 0, near)
     rs_two(f, 1)
+    join(r, 1)
     back(r, 0, far)
     pl.semaphore_wait(credit.at[r], 2)
     rs_begin(r, 0)
     rs_one(f, 1)
-    join(r, 1)
     rs_pass(f, 1)
+    lower(r, 1, near)
     back(r, 0, near)
-    lower(r, 1, near)
+    rs_end(f, 0)
     rs_two(r, 0)
     rs_one(r, 0)
     back(r, 1, far)
     rs_begin(r, 1)
+    back(r, 1, near)
     rs_pass(r, 0)
-    back(r, 1, near)
     rs_two(r, 1)
+    rs_end(f, 1)
     rs_one(r, 1)
     rs_pass(r, 1)
     rs_end(r, 0)
-    rs_end(f, 1)
     rs_end(r, 1)
     for i in range(len(INFO)):
         inf_copy(i).wait_send()

time: 271 us -> 271 us (level)
  no operation moved by 1% of the time
where the time goes in v7:
time: 271 us
  Pallas kernels  269 us (99%)
    pallas_call x1, Pallas kernels, shards(): pl.pallas_call(functools.partial(kernel, cap), out_shape=(pltpu.VMEM((tok...  269 us

profile of v7, /device:TPU:1, one launch (start us, length us, event | category | flops | bytes accessed | tf_op | source)
XLA Modules:
  0.0 271.0 jit_solution(10655892530030320417)
XLA Ops:
  0.6 268.5 %shard_map.86 = (bf16[128,3584]{1,0:T(8,128)(2,1)S(1)}, bf16[128,3584]{1,0:T(8,128)(2,1)S(1)}) custom-call(bf16[128,3584]{1,0:T(8,128)(2,1)} %bitcast.16, bf16[128,3584]{1,0:T(8,128)(2,1)} %bitcast.17, bf16[1,3584]{1,0:T(2,128)(2,1)} %gain_ref.1, bf16[3584,512]{1,0:T(8,128)(2,1)} %bitcast.14, bf16[512,3584]{1,0:T(8,128)(2,1)} %bitcast.15, ...), custom_call_target="tpu_custom_call" | custom-call | flops 9395240960 | bytes 16777216 | tf_op jit(solution)/shard_map/pallas_call | solution.py:603
  269.2 0.9 copy.11
  270.1 0.9 copy.12
